TPU v7x, 128 devices: a whole 4x4x4 slice. The times are simulated.
128 devices in a mesh: row: 32 (over x_hi, y, z), col: 4 (over x_lo, core).
Axes of the slice: x: 4 (x_hi: 2, x_lo: 2; x = x_hi * 2 + x_lo), y: 4, z: 4, core: 2. Of those that a mesh axis runs over, the one named last changes fastest.
Arguments:
- atom_feats: bfloat16 [20480, 128], P('row'), may hold values from -6 to 6
- atom_gain: float32 [128], replicated, may hold values from 0.1 to 1.9
- w_atom: bfloat16 [3, 128, 128], P(None, None, 'col'), may hold values from -0.5 to 0.5
- atom_pair: bfloat16 [16, 20480, 128], P(None, 'row'), may hold values from -80 to 80
- w_atom_bias: bfloat16 [16, 4], P(None, 'col'), may hold values from -2 to 2
- atom_counts: int32 [2560], P('row'), may hold values from 2 to 24, as said below
- token_single: bfloat16 [2560, 768], P('row'), may hold values from -3 to 3
- w_pool: bfloat16 [128, 768], replicated, may hold values from -2 to 2
- token_gain: float32 [2, 768], replicated, may hold values from 0.1 to 1.9
- w_attn: bfloat16 [2, 4, 768, 768], P(None, None, None, 'col'), may hold values from -0.21875 to 0.21875
- w_out: bfloat16 [2, 768, 768], P(None, 'col'), may hold values from -0.21875 to 0.21875
- pair: bfloat16 [2560, 2560, 128], P('row', 'col'), may hold values from -30 to 30
- w_bias: bfloat16 [2, 128, 16], replicated, may hold values from -1 to 1
Outputs:
- tokens_out: bfloat16 [2560, 768], P('row')
Inputs may be any that keep to these rules, and one draw needn't show every extreme that they name: `atom_counts`: the first 640 tokens have 24 atoms each, every other token 2 or 3; counts sum to 20480.
All inputs are finite; a program needn't handle non-finite values.
Results may differ from a plain program's by a relative error of at most 0.02.
Values may be sent and summed in bfloat16 or wider, within the bound.
No kernel may reach another device: no remote copies, remote signals or barrier semaphores. Data moves between devices by JAX's collectives and lax.ppermute only.
A program may use at most 128 MiB of HBM per device.

v0:
```python
import functools
import math

import jax
import jax.numpy as jnp
from jax import lax
from jax.experimental import pallas as pl
from jax.experimental.pallas import tpu as pltpu
from jax.sharding import PartitionSpec as P

QBLOCK = 32
WK = 128
REACH = 48
EPSILON = 1e-05
NC = 4
TOP, LANES = 16, 128
BF = jnp.bfloat16
F32 = jnp.float32
VMEM_LIMIT = 16 * 1024 * 1024
NT = (((1,), (1,)), ((), ()))
TN = (((0,), (0,)), ((), ()))


def dot(a, b, dims=(((1,), (0,)), ((), ()))):
    return lax.dot_general(a, b, dims, preferred_element_type=F32)


def layer_norm(values, gain_row):
    centred = values - jnp.mean(values, axis=-1, keepdims=True)
    spread = jnp.mean(centred * centred, axis=-1, keepdims=True)
    return centred * lax.rsqrt(spread + EPSILON) * gain_row


def call(kernel, out_shape, flops, moved, **kw):
    return pl.pallas_call(
        kernel,
        out_shape=out_shape,
        compiler_params=pltpu.CompilerParams(vmem_limit_bytes=VMEM_LIMIT),
        cost_estimate=pl.CostEstimate(flops=flops, bytes_accessed=moved, transcendentals=0),
        **kw,
    )


def shaped(shape, dtype):
    return jax.ShapeDtypeStruct(shape, dtype)


def pair_bias_kernel(col_ref, pair_ref, w_ref, *out_refs):
    total, own = w_ref.shape[0], out_refs[0].shape[0]
    to = lax.broadcasted_iota(jnp.int32, (total, total), 0)
    at = lax.broadcasted_iota(jnp.int32, (total, total), 1)
    heads = NC * own
    wanted = to // heads * heads + ((to % heads // own) ^ col_ref[0]) * own + to % own
    w = dot(jnp.where(at == wanted, 1.0, 0.0).astype(BF), w_ref[...]).astype(BF)
    for i in range(pair_ref.shape[0]):
        bias = dot(w, pair_ref[i], NT).astype(BF)
        for at, out_ref in enumerate(out_refs):
            out_ref[:, i, :] = bias[at * own : (at + 1) * own]


def pair_bias_call(col_at, pair, w_t, layers):
    rows, cols, ch = pair.shape
    own = w_t.shape[0] // (layers * NC)
    step = 16
    return pl.pallas_call(
        pair_bias_kernel,
        grid=(rows // step,),
        in_specs=[
            smem(),
            pl.BlockSpec((step, cols, ch), lambda i: (i, 0, 0)),
            pl.BlockSpec(w_t.shape, lambda i: (0, 0)),
        ],
        out_specs=[pl.BlockSpec((own, step, cols), lambda i: (0, i, 0))] * (layers * NC),
        out_shape=[shaped((own, rows, cols), BF)] * (layers * NC),
        compiler_params=pltpu.CompilerParams(vmem_limit_bytes=56 * 1024 * 1024),
        cost_estimate=pl.CostEstimate(
            flops=64 * rows * cols * ch, bytes_accessed=2 * rows * cols * (ch + 32), transcendentals=0
        ),
    )(col_at, pair, w_t)


def pack_kernel(row_ref, feats_ref, counts_ref, out_ref):
    rows = out_ref.shape[0]
    tq = counts_ref.shape[1]
    last = feats_ref.shape[0] - REACH
    counts = counts_ref[...].astype(F32)
    counts = jnp.concatenate([counts, jnp.zeros((1, LANES - tq), F32)], axis=1)
    top = jnp.where(lax.broadcasted_iota(jnp.int32, (TOP, LANES), 0) == 0, counts, 0.0).astype(BF)
    head = feats_ref[:REACH]
    for d in range(rows):
        out_ref[d, :TOP] = top
        out_ref[d, TOP:] = head

    @pl.when(row_ref[0] + 1 < rows)
    def _():
        out_ref[row_ref[0] + 1, TOP:] = feats_ref[last:]


def atom_kernel(row_ref, msg_ref, feats_ref, gain_ref, w_ref, wab_ref, apair_ref, out_ref, own_ref, counts_ref):
    rows = feats_ref.shape[0]
    n_rows = msg_ref.shape[0]
    tq = out_ref.shape[2]
    row = row_ref[0]
    first = row * rows
    total = rows * n_rows
    prev = msg_ref[jnp.maximum(row - 1, 0), TOP:]
    nxt = msg_ref[jnp.minimum(row + 1, n_rows - 1), TOP:]
    x = jnp.concatenate([prev, feats_ref[...], nxt], axis=0).astype(F32)
    normed = layer_norm(x, gain_ref[...]).astype(BF)
    q = dot(normed[REACH : REACH + rows], w_ref[0], NT).astype(BF)
    k = dot(normed, w_ref[1], NT).astype(BF)
    v = dot(normed, w_ref[2], NT).astype(BF)
    wab = wab_ref[...].astype(F32).T
    bias = apair_ref[0].astype(F32) * wab[0:1, 0:1]
    for c in range(1, apair_ref.shape[0]):
        bias += apair_ref[c].astype(F32) * wab[c : c + 1, 0:1]
    scores = jnp.concatenate(
        [dot(q[at : at + QBLOCK], k[at : at + WK], NT) for at in range(0, rows, QBLOCK)], axis=0
    )
    scores = scores * (1.0 / math.sqrt(q.shape[1])) + bias
    at = lax.broadcasted_iota(jnp.int32, (rows, WK), 0) // QBLOCK * QBLOCK
    key_at = at + lax.broadcasted_iota(jnp.int32, (rows, WK), 1) + (first - REACH)
    scores = jnp.where((key_at >= 0) & (key_at < total), scores, -1e30)
    weights = jnp.exp(scores - jnp.max(scores, axis=-1, keepdims=True))
    probs = (weights / jnp.sum(weights, axis=-1, keepdims=True)).astype(BF)
    out = jnp.concatenate(
        [dot(probs[at : at + QBLOCK], v[at : at + WK]) for at in range(0, rows, QBLOCK)], axis=0
    )
    out_t = out.T.astype(BF)

    counts = jnp.sum(msg_ref[:, :TOP].astype(F32), axis=1)
    small = counts.astype(BF)
    upto = lax.broadcasted_iota(jnp.int32, (LANES, LANES), 0) <= lax.broadcasted_iota(jnp.int32, (LANES, LANES), 1)
    inside = dot(small, jnp.where(upto, 1.0, 0.0).astype(BF))
    below = lax.broadcasted_iota(jnp.int32, (n_rows, n_rows), 1) < lax.broadcasted_iota(jnp.int32, (n_rows, n_rows), 0)
    before = jnp.sum(dot(jnp.where(below, 1.0, 0.0).astype(BF), small), axis=1, keepdims=True)
    ends = before + inside
    starts = ends - counts
    index = (lax.broadcasted_iota(jnp.int32, (rows, tq), 0) + first).astype(F32)
    for part in range(n_rows):
        start, end = starts[part : part + 1, :tq], ends[part : part + 1, :tq]
        member = jnp.where((index >= start) & (index < end), 1.0, 0.0).astype(BF)
        out_ref[part] = dot(out_t, member).astype(BF)
    counts_ref[...] = counts
    own_ref[...] = counts_ref[pl.ds(row, 1), :tq]


def sums_kernel(parts_ref, out_ref):
    sums = parts_ref[0].astype(F32)
    for part in range(1, parts_ref.shape[0]):
        sums += parts_ref[part].astype(F32)
    out_ref[...] = sums.astype(BF)


def smem():
    return pl.BlockSpec(memory_space=pltpu.SMEM)


def vmem():
    return pl.BlockSpec(memory_space=pltpu.VMEM)


def project(residual, gain, w_ref, kv_ref, qg_ref):
    width = w_ref.shape[2]
    normed = layer_norm(residual, gain).astype(BF)
    kv_ref[...] = dot(normed, w_ref[0, 1:3].reshape(2 * width, -1), NT).astype(BF)
    qg_ref[0] = dot(normed, w_ref[0, 0], NT).astype(BF)
    qg_ref[1] = dot(normed, w_ref[0, 3], NT).astype(BF)


def first_kernel(sums_ref, counts_ref, single_ref, w_pool_ref, gain_ref, w_ref, res_ref, kv_ref, qg_ref):
    pooled = (sums_ref[...].astype(F32) / counts_ref[...]).astype(BF)
    residual = single_ref[...].astype(F32) + dot(pooled, w_pool_ref[...], TN)
    res_ref[...] = residual
    project(residual, gain_ref[0:1], w_ref, kv_ref, qg_ref)


def spread_kernel(own_ref, far_ref, out_ref):
    for d in range(out_ref.shape[0]):
        out_ref[d, 0] = own_ref[...]
        out_ref[d, 1] = far_ref[...]


def attend_kernel(col_ref, half_ref, qg_ref, kv_ref, bias0_ref, bias1_ref, bias2_ref, bias3_ref, out_ref):
    own, rows, cols = bias0_ref.shape
    width = qg_ref.shape[2]
    hd = width // own
    wide = 2 * LANES
    skip = 2 * width - wide
    per = cols // rows
    lane = lax.broadcasted_iota(jnp.int32, (rows, wide), 1)
    q = jnp.concatenate([qg_ref[0], jnp.zeros((rows, wide - width), BF)], axis=1)
    q = jnp.concatenate(
        [jnp.where((lane >= h * hd) & (lane < (h + 1) * hd), q, jnp.zeros_like(q)) for h in range(own)], axis=0
    )
    scores, values = [], []
    for step, bias_ref in enumerate((bias0_ref, bias1_ref, bias2_ref, bias3_ref)):
        block = col_ref[0] ^ step
        at = block * per
        half = at // kv_ref.shape[0]
        kv = kv_ref[pl.ds(at - half * kv_ref.shape[0], per), half ^ half_ref[0]].reshape(cols, 2 * width)
        values.append(kv[:, skip:])
        part = dot(q, kv[:, :wide], NT) * (1.0 / math.sqrt(hd))
        scores.append(part + bias_ref[...].reshape(own * rows, cols).astype(F32))
    top = functools.reduce(jnp.maximum, [jnp.max(part, axis=-1, keepdims=True) for part in scores])
    weights = [jnp.exp(part - top) for part in scores]
    share = 1.0 / sum(jnp.sum(part, axis=-1, keepdims=True) for part in weights)
    mixture = sum(dot((part * share).astype(BF), v) for part, v in zip(weights, values))
    lane = lane - (wide - width)
    out = jnp.zeros((rows, wide), F32)
    for h in range(own):
        out = jnp.where((lane >= h * hd) & (lane < (h + 1) * hd), mixture[h * rows : (h + 1) * rows], out)
    out_ref[...] = (out[:, wide - width :] * jax.nn.sigmoid(qg_ref[1].astype(F32))).astype(BF)


def out_rows(col_ref, gated_ref, w_out_refs):
    return sum(dot(gated_ref[col_ref[0] ^ step], w_ref[...]) for step, w_ref in enumerate(w_out_refs))


def middle_kernel(col_ref, res_ref, gated_ref, w0_ref, w1_ref, w2_ref, w3_ref, gain_ref, w_ref, out_ref, kv_ref, qg_ref):
    residual = res_ref[...] + out_rows(col_ref, gated_ref, (w0_ref, w1_ref, w2_ref, w3_ref))
    out_ref[...] = residual
    project(residual, gain_ref[1:2], w_ref, kv_ref, qg_ref)


def last_kernel(col_ref, res_ref, gated_ref, w0_ref, w1_ref, w2_ref, w3_ref, out_ref):
    out_ref[...] = (res_ref[...] + out_rows(col_ref, gated_ref, (w0_ref, w1_ref, w2_ref, w3_ref))).astype(BF)


def exchange(x, axis):
    return lax.all_to_all(x, axis, 0, 0, tiled=True)


def from_step(x, step):
    return lax.ppermute(x, "col", [(i, i ^ step) for i in range(NC)])


def on_device(
    atom_feats, atom_gain, w_atom, atom_pair, w_atom_bias, atom_counts, token_single,
    w_pool, token_gain, w_attn, w_out, pair, w_bias,
):
    n_rows = lax.axis_size("row")
    half = n_rows // 2
    halves = [list(range(half)), list(range(half, n_rows))]
    row_at = lax.axis_index("row").astype(jnp.int32)[None]
    half_at = row_at // half
    col_at = lax.axis_index("col").astype(jnp.int32)[None]
    atom_rows, width_a = atom_feats.shape
    tq, ct = token_single.shape
    layers, ch, heads = w_bias.shape
    width = w_attn.shape[3]
    own = heads // NC

    msg = call(pack_kernel, shaped((n_rows, TOP + REACH, LANES), BF), 0, 1 << 19, in_specs=[smem(), vmem(), vmem()], out_specs=vmem())(
        row_at, atom_feats, atom_counts[None]
    )
    msg = exchange(msg, "row")

    w_t = w_bias.transpose(0, 2, 1).reshape(layers * heads, ch)
    local_bias = pair_bias_call(col_at, pair, w_t, layers)
    msg, *local_bias = lax.optimization_barrier((msg, *local_bias))

    head_a = w_atom.shape[2]
    partial, own_counts = call(
        atom_kernel,
        [shaped((n_rows, head_a, tq), BF), shaped((1, tq), F32)],
        2 * atom_rows * (3 * width_a * head_a + 2 * WK * head_a + head_a * n_rows * tq),
        2 * atom_pair.size,
        in_specs=[smem()] + [vmem()] * 6,
        out_specs=[vmem()] * 2,
        scratch_shapes=[pltpu.VMEM((n_rows, LANES), F32)],
    )(row_at, msg, atom_feats, atom_gain[None], w_atom.transpose(0, 2, 1), w_atom_bias.T, atom_pair)
    sums = call(sums_kernel, shaped((head_a, tq), BF), 0, 1 << 18)(exchange(partial, "row"))
    sums = lax.all_gather(sums, "col", axis=0, tiled=True)

    w_attn_t = w_attn.transpose(0, 1, 3, 2)
    proj = [shaped((tq, ct), F32), shaped((tq, 2 * width), BF), shaped((2, tq, width), BF)]

    def w_spec(l):
        return pl.BlockSpec((1, 4, width, ct), lambda i: (l, 0, 0, 0))

    residual, kv, qg = call(
        first_kernel, proj, 2 * tq * ct * ct, 2 * ct * ct,
        grid=(1,), in_specs=[vmem()] * 5 + [w_spec(0)], out_specs=[vmem()] * 3,
    )(sums, own_counts, token_single, w_pool, token_gain, w_attn_t)
    for l in range(layers):
        far = lax.ppermute(kv, "row", [(i, (i + half) % n_rows) for i in range(n_rows)])
        pieces = local_bias[l * NC : (l + 1) * NC]
        kv, far, w_own, *pieces = lax.optimization_barrier((kv, far, w_out[l], *pieces))
        kv = call(spread_kernel, shaped((half, 2) + kv.shape, BF), 0, 4 * half * kv.size, in_specs=[vmem()] * 2, out_specs=vmem())(
            kv, far
        )
        w_far = from_step(w_own, 2)
        now = [pieces[0]] + [from_step(pieces[step], step) for step in range(1, NC)]
        moved = [from_step(w_own, 1), w_far, from_step(w_far, 1)]
        kv = lax.all_to_all(kv, "row", 0, 0, tiled=True, axis_index_groups=halves)
        kv, *moved = lax.optimization_barrier((kv, *moved))
        w_outs = [w_own] + moved
        gated = call(
            attend_kernel, shaped((tq, width), BF), 4 * tq * n_rows * tq * width, 2 * heads * tq * n_rows * tq // NC,
            in_specs=[smem()] * 2 + [vmem()] * 6, out_specs=vmem(),
        )(col_at, half_at, qg, kv, *now)
        gated = lax.all_gather(gated, "col", axis=0, tiled=False)
        if l + 1 < layers:
            residual, kv, qg = call(
                middle_kernel, proj, 4 * tq * ct * ct, 4 * ct * ct,
                grid=(1,),
                in_specs=[smem()] + [vmem()] * 7 + [w_spec(l + 1)],
                out_specs=[vmem()] * 3,
            )(col_at, residual, gated, *w_outs, token_gain, w_attn_t)
    return call(
        last_kernel, shaped((tq, ct), BF), 2 * tq * ct * ct, 2 * ct * ct,
        in_specs=[smem()] + [vmem()] * 6, out_specs=vmem(),
    )(col_at, residual, gated, *w_outs)


def solution(mesh):
    placed = (
        P("row", None),
        P(),
        P(None, None, "col"),
        P(None, "row", None),
        P(None, "col"),
        P("row"),
        P("row", None),
        P(),
        P(),
        P(None, None, None, "col"),
        P(None, "col", None),
        P("row", "col", None),
        P(),
    )
    return jax.shard_map(
        on_device, mesh=mesh, in_specs=placed, out_specs=P("row", None), check_vma=False
    )
```

profile of v0, /device:TPU:1, one launch (start us, length us, event | category | flops | bytes accessed | tf_op | source)
XLA Modules:
  0.0 159.3 jit_solution(7626563137871417086)
XLA Ops:
  2.5 11.3 %all-to-all-start = ((bf16[32,64,128]{2,1,0:T(8,128)(2,1)}), bf16[32,64,128]{2,1,0:T(8,128)(2,1)S(1)}, u32[]{:S(2)}, u32[]{:S(2)}) async-start(bf16[32,64,128]{2,1,0:T(8,128)(2,1)} %shard_map.127), calls=%async_computation | async-start | bytes 1048576 | tf_op jit(solution)/shard_map/all_to_all | solution.py:231
  13.9 10.3 %shard_map.128 = (bf16[4,80,640]{2,1,0:T(8,128)(2,1)}, bf16[4,80,640]{2,1,0:T(8,128)(2,1)}, bf16[4,80,640]{2,1,0:T(8,128)(2,1)}, bf16[4,80,640]{2,1,0:T(8,128)(2...) custom-call(s32[1]{0:T(128)} %bitcast.col_ref, ...), custom_call_target="tpu_custom_call" | custom-call | flops 419430400 | bytes 16384000 | tf_op jit(solution)/shard_map/pallas_call | solution.py:65
  25.0 1.7 %copy-done.3 = bf16[16,640,128]{2,1,0:T(8,128)(2,1)S(1)} copy-done((bf16[16,640,128]{2,1,0:T(8,128)(2,1)S(1)}, bf16[16,640,128]{2,1,0:T(8,128)(2,1)}, u32[]{:S(2)}) %copy-start.3) | copy-done | bytes 2621464
  26.8 3.0 %shard_map.129 = (bf16[32,32,80]{2,1,0:T(8,128)(2,1)S(1)}, f32[1,80]{1,0:T(1,128)S(1)}) custom-call(s32[1]{0:T(128)} %bitcast.1.row_ref, bf16[32,64,128]{2,1,0:T(8,128)(2,1)S(1)} %all-to-all-done.msg_ref, bf16[640,128]{1,0:T(8,128)(2,1)S(1)} %copy-done.5, f32[1,128]{1,0:T(1,128)S(1)} %bitcast.22, bf16[3,32,128]{2,1,0:T(8,128)(2,1)S(1)} %bitcast.20, ...), custom_call_target="tpu_custom_call" | custom-call | flops 131072000 | bytes 2621440 | tf_op jit(solution)/shard_map/pallas_call | solution.py:264
  29.8 17.9 %all_to_all.20.parts_ref = bf16[32,32,80]{2,1,0:T(8,128)(2,1)S(1)} all-to-all(bf16[32,32,80]{2,1,0:T(8,128)(2,1)S(1)} %get-tuple-element.61), channel_id=1, replica_groups=mesh['row'=32,'col'=4] {'row'}, dimensions={0} | all-to-all | bytes 327680 | tf_op jit(solution)/shard_map/all_to_all | solution.py:231
  47.8 7.7 %all_gather.15.sums_ref = bf16[128,80]{1,0:T(8,128)(2,1)S(1)} all-gather(bf16[32,80]{1,0:T(8,128)(2,1)S(1)} %shard_map.130), channel_id=1, replica_groups=mesh['row'=32,'col'=4] {'col'}, dimensions={0}, use_global_device_ids=true | all-gather | bytes 25600 | tf_op jit(solution)/shard_map/all_gather | solution.py:274
  56.9 4.4 %collective-permute-done.far_ref = bf16[80,384]{1,0:T(8,128)(2,1)S(1)} collective-permute-done((bf16[80,384]{1,0:T(8,128)(2,1)S(1)}, bf16[80,384]{1,0:T(8,128)(2,1)S(1)}, u32[]{:S(2)}, u32[]{:S(2)}) %collective-permute-start) | collective-permute-done | bytes 61472 | tf_op jit(solution)/shard_map/ppermute | solution.py:287
  61.5 1.3 copy-done.1
  62.8 4.6 %all-to-all-start.2 = ((bf16[16,2,80,384]{3,2,1,0:T(8,128)(2,1)}), bf16[16,2,80,384]{3,2,1,0:T(8,128)(2,1)}, u32[]{:S(2)}, u32[]{:S(2)}) async-start(bf16[16,2,80,384]{3,2,1,0:T(8,128)(2,1)} %copy-done.1), calls=%async_computation.2 | async-start | bytes 3932160 | tf_op jit(solution)/shard_map/all_to_all | solution.py:296
  67.8 1.3 collective-permute-start.4
  70.9 4.2 %collective-permute-done.2.w2_ref = bf16[192,768]{1,0:T(8,128)(2,1)S(1)} collective-permute-done((bf16[192,768]{1,0:T(8,128)(2,1)S(1)}, bf16[192,768]{1,0:T(8,128)(2,1)S(1)}, u32[]{:S(2)}, u32[]{:S(2)}) %collective-permute-start.2) | collective-permute-done | bytes 294944 | tf_op jit(solution)/shard_map/ppermute | solution.py:235
  75.1 3.3 %collective-permute-start.3 = (bf16[192,768]{1,0:T(8,128)(2,1)S(1)}, bf16[192,768]{1,0:T(8,128)(2,1)S(1)}, u32[]{:S(2)}, u32[]{:S(2)}) collective-permute-start(bf16[192,768]{1,0:T(8,128)(2,1)S(1)} %collective-permute-done.2.w2_ref), channel_id=1, source_target_pairs={{0,1},{1,0},{2,3},{3,2},{4,5},{5,4},{6,7},{7,6},{8,9},{9,8},{10,11... | collective-permute-start | bytes 884744 | tf_op jit(solution)/shard_map/ppermute | solution.py:235
  80.6 12.5 %all-to-all-done.2.kv_ref = bf16[16,2,80,384]{3,2,1,0:T(8,128)(2,1)} async-done(((bf16[16,2,80,384]{3,2,1,0:T(8,128)(2,1)}), bf16[16,2,80,384]{3,2,1,0:T(8,128)(2,1)}, u32[]{:S(2)}, u32[]{:S(2)}) %all-to-all-start.2) | async-done | bytes 1966112 | tf_op jit(solution)/shard_map/all_to_all | solution.py:296
  94.2 4.7 %shard_map.133 = bf16[80,192]{1,0:T(8,128)(2,1)S(1)} custom-call(s32[1]{0:T(128)} %bitcast.col_ref, s32[1]{0:T(128)S(6)} %select_n.5.half_ref, bf16[2,80,192]{2,1,0:T(8,128)(2,1)S(1)} %get-tuple-element.64.qg_ref, bf16[16,2,80,384]{3,2,1,0:T(8,128)(2,1)} %all-to-all-done.2.kv_ref, bf16[4,80,640]{2,1,0:T(8,128)(2,1)S(1)} %copy-done.7, ...), custom_call_target="tpu_custom_call" | custom-call | flops 157286400 | bytes 1638400 | tf_op jit(solution)/shard_map/pallas_call | solution.py:299
  98.9 8.2 %all-gather = bf16[320,192]{1,0:T(8,128)(2,1)S(1)} all-gather(bf16[80,192]{1,0:T(8,128)(2,1)S(1)} %shard_map.133), channel_id=2, replica_groups=mesh['row'=32,'col'=4] {'col'}, dimensions={0}, use_global_device_ids=true | all-gather | bytes 153600 | tf_op jit(solution)/shard_map/all_gather | solution.py:303
  109.3 4.5 %collective-permute-done.7.far_ref = bf16[80,384]{1,0:T(8,128)(2,1)S(1)} collective-permute-done((bf16[80,384]{1,0:T(8,128)(2,1)S(1)}, bf16[80,384]{1,0:T(8,128)(2,1)S(1)}, u32[]{:S(2)}, u32[]{:S(2)}) %collective-permute-start.7) | collective-permute-done | bytes 61472 | tf_op jit(solution)/shard_map/ppermute | solution.py:287
  114.0 1.3 copy-done.2
  115.3 4.0 %all-to-all-start.3 = ((bf16[16,2,80,384]{3,2,1,0:T(8,128)(2,1)}), bf16[16,2,80,384]{3,2,1,0:T(8,128)(2,1)S(1)}, u32[]{:S(2)}, u32[]{:S(2)}) async-start(bf16[16,2,80,384]{3,2,1,0:T(8,128)(2,1)} %copy-done.2), calls=%async_computation.3 | async-start | bytes 3932160 | tf_op jit(solution)/shard_map/all_to_all | solution.py:296
  119.7 1.2 collective-permute-start.11
  122.9 4.1 %collective-permute-done.9.w2_ref = bf16[192,768]{1,0:T(8,128)(2,1)S(1)} collective-permute-done((bf16[192,768]{1,0:T(8,128)(2,1)S(1)}, bf16[192,768]{1,0:T(8,128)(2,1)S(1)}, u32[]{:S(2)}, u32[]{:S(2)}) %collective-permute-start.9) | collective-permute-done | bytes 294944 | tf_op jit(solution)/shard_map/ppermute | solution.py:235
  126.9 3.4 %collective-permute-start.10 = (bf16[192,768]{1,0:T(8,128)(2,1)S(1)}, bf16[192,768]{1,0:T(8,128)(2,1)S(1)}, u32[]{:S(2)}, u32[]{:S(2)}) collective-permute-start(bf16[192,768]{1,0:T(8,128)(2,1)S(1)} %collective-permute-done.9.w2_ref), channel_id=1, source_target_pairs={{0,1},{1,0},{2,3},{3,2},{4,5},{5,4},{6,7},{7,6},{8,9},{9,8},{10,11... | collective-permute-start | bytes 884744 | tf_op jit(solution)/shard_map/ppermute | solution.py:235
  132.4 12.7 %all-to-all-done.3.kv_ref = bf16[16,2,80,384]{3,2,1,0:T(8,128)(2,1)S(1)} async-done(((bf16[16,2,80,384]{3,2,1,0:T(8,128)(2,1)}), bf16[16,2,80,384]{3,2,1,0:T(8,128)(2,1)S(1)}, u32[]{:S(2)}, u32[]{:S(2)}) %all-to-all-start.3) | async-done | bytes 1966112 | tf_op jit(solution)/shard_map/all_to_all | solution.py:296
  146.0 4.0 %shard_map.136 = bf16[80,192]{1,0:T(8,128)(2,1)S(1)} custom-call(s32[1]{0:T(128)} %bitcast.col_ref, s32[1]{0:T(128)S(6)} %select_n.5.half_ref, bf16[2,80,192]{2,1,0:T(8,128)(2,1)S(1)} %get-tuple-element.82.qg_ref, bf16[16,2,80,384]{3,2,1,0:T(8,128)(2,1)S(1)} %all-to-all-done.3.kv_ref, bf16[4,80,640]{2,1,0:T(8,128)(2,1)S(1)} %copy-done.6, ...), custom_call_target="tpu_custom_call" | custom-call | flops 157286400 | bytes 1638400 | tf_op jit(solution)/shard_map/pallas_call | solution.py:299
  150.0 8.3 %all-gather.1 = bf16[320,192]{1,0:T(8,128)(2,1)S(1)} all-gather(bf16[80,192]{1,0:T(8,128)(2,1)S(1)} %shard_map.136), channel_id=3, replica_groups=mesh['row'=32,'col'=4] {'col'}, dimensions={0}, use_global_device_ids=true | all-gather | bytes 153600 | tf_op jit(solution)/shard_map/all_gather | solution.py:303
  (90 shorter events, 19.1 us)
Async XLA Ops:
  2.5 22.5 %all-to-all-start = ((bf16[32,64,128]{2,1,0:T(8,128)(2,1)}), bf16[32,64,128]{2,1,0:T(8,128)(2,1)S(1)}, u32[]{:S(2)}, u32[]{:S(2)}) async-start(bf16[32,64,128]{2,1,0:T(8,128)(2,1)} %shard_map.127), calls=%async_computation | async-start | bytes 1048576 | tf_op jit(solution)/shard_map/all_to_all | solution.py:231
  26.7 28.7 %copy-start = (bf16[2,4,768,192]{2,3,1,0:T(8,128)(2,1)S(1)}, bf16[2,4,768,192]{2,3,1,0:T(8,128)(2,1)}, u32[]{:S(2)}) copy-start(bf16[2,4,768,192]{2,3,1,0:T(8,128)(2,1)} %param.22) | copy-start | bytes 7077892
  26.7 28.7 %copy-start.24 = (bf16[128,768]{1,0:T(8,128)(2,1)S(1)}, bf16[128,768]{1,0:T(8,128)(2,1)}, u32[]{:S(2)}) copy-start(bf16[128,768]{1,0:T(8,128)(2,1)} %w_pool_ref.1) | copy-start | bytes 589828
  26.7 28.7 %copy-start.25 = (bf16[80,768]{1,0:T(8,128)(2,1)S(1)}, bf16[80,768]{1,0:T(8,128)(2,1)}, u32[]{:S(2)}) copy-start(bf16[80,768]{1,0:T(8,128)(2,1)} %single_ref.1) | copy-start | bytes 368644
  26.7 28.7 %copy-start.27 = (f32[2,768]{1,0:T(2,128)S(1)}, f32[2,768]{1,0:T(2,128)}, u32[]{:S(2)}) copy-start(f32[2,768]{1,0:T(2,128)} %gain_ref.3) | copy-start | bytes 18436
  29.8 27.1 %copy-start.31 = (bf16[2,192,768]{2,1,0:T(8,128)(2,1)S(1)}, bf16[2,192,768]{2,1,0:T(8,128)(2,1)}, u32[]{:S(2)}) copy-start(bf16[2,192,768]{2,1,0:T(8,128)(2,1)} %param.23) | copy-start | bytes 1769476
  56.3 5.0 %collective-permute-start = (bf16[80,384]{1,0:T(8,128)(2,1)S(1)}, bf16[80,384]{1,0:T(8,128)(2,1)S(1)}, u32[]{:S(2)}, u32[]{:S(2)}) collective-permute-start(bf16[80,384]{1,0:T(8,128)(2,1)S(1)} %get-tuple-element.70.own_ref), channel_id=1, source_target_pairs={{0,64},{4,68},{8,72},{12,76},{16,80},{20,84},{24,88},{28,92},{32,9... | collective-permute-start | bytes 184328 | tf_op jit(solution)/shard_map/ppermute | solution.py:287
  62.8 31.3 %copy-start.7 = (bf16[4,80,640]{2,1,0:T(8,128)(2,1)S(1)}, bf16[4,80,640]{2,1,0:T(8,128)(2,1)}, u32[]{:S(2)}) copy-start(bf16[4,80,640]{2,1,0:T(8,128)(2,1)} %get-tuple-element.74.bias0_ref) | copy-start | bytes 1228804
  62.8 30.2 %all-to-all-start.2 = ((bf16[16,2,80,384]{3,2,1,0:T(8,128)(2,1)}), bf16[16,2,80,384]{3,2,1,0:T(8,128)(2,1)}, u32[]{:S(2)}, u32[]{:S(2)}) async-start(bf16[16,2,80,384]{3,2,1,0:T(8,128)(2,1)} %copy-done.1), calls=%async_computation.2 | async-start | bytes 3932160 | tf_op jit(solution)/shard_map/all_to_all | solution.py:296
  67.4 7.7 %collective-permute-start.2 = (bf16[192,768]{1,0:T(8,128)(2,1)S(1)}, bf16[192,768]{1,0:T(8,128)(2,1)S(1)}, u32[]{:S(2)}, u32[]{:S(2)}) collective-permute-start(bf16[192,768]{1,0:T(8,128)(2,1)S(1)} %get-tuple-element.72.w0_ref), channel_id=1, source_target_pairs={{0,2},{1,3},{2,0},{3,1},{4,6},{5,7},{6,4},{7,5},{8,10},{9,11},{10,... | collective-permute-start | bytes 884744 | tf_op jit(solution)/shard_map/ppermute | solution.py:235
  67.8 25.3 %collective-permute-start.4 = (bf16[4,80,640]{2,1,0:T(8,128)(2,1)}, bf16[4,80,640]{2,1,0:T(8,128)(2,1)}, u32[]{:S(2)}, u32[]{:S(2)}) collective-permute-start(bf16[4,80,640]{2,1,0:T(8,128)(2,1)} %get-tuple-element.75), channel_id=1, source_target_pairs={{0,1},{1,0},{2,3},{3,2},{4,5},{5,4},{6,7},{7,6},{8,9},{9,8},{10,11... | collective-permute-start | bytes 1228808 | tf_op jit(solution)/shard_map/ppermute | solution.py:235
  69.0 24.0 %collective-permute-start.5 = (bf16[4,80,640]{2,1,0:T(8,128)(2,1)}, bf16[4,80,640]{2,1,0:T(8,128)(2,1)}, u32[]{:S(2)}, u32[]{:S(2)}) collective-permute-start(bf16[4,80,640]{2,1,0:T(8,128)(2,1)} %get-tuple-element.76), channel_id=1, source_target_pairs={{0,2},{1,3},{2,0},{3,1},{4,6},{5,7},{6,4},{7,5},{8,10},{9,11},{10,... | collective-permute-start | bytes 1228808 | tf_op jit(solution)/shard_map/ppermute | solution.py:235
  70.2 23.9 %collective-permute-start.6 = (bf16[4,80,640]{2,1,0:T(8,128)(2,1)}, bf16[4,80,640]{2,1,0:T(8,128)(2,1)}, u32[]{:S(2)}, u32[]{:S(2)}) collective-permute-start(bf16[4,80,640]{2,1,0:T(8,128)(2,1)} %get-tuple-element.77), channel_id=1, source_target_pairs={{0,3},{1,2},{2,1},{3,0},{4,7},{5,6},{6,5},{7,4},{8,11},{9,10},{10,... | collective-permute-start | bytes 1228808 | tf_op jit(solution)/shard_map/ppermute | solution.py:235
  70.7 8.4 %collective-permute-start.1 = (bf16[192,768]{1,0:T(8,128)(2,1)S(1)}, bf16[192,768]{1,0:T(8,128)(2,1)S(1)}, u32[]{:S(2)}, u32[]{:S(2)}) collective-permute-start(bf16[192,768]{1,0:T(8,128)(2,1)S(1)} %get-tuple-element.72.w0_ref), channel_id=1, source_target_pairs={{0,1},{1,0},{2,3},{3,2},{4,5},{5,4},{6,7},{7,6},{8,9},{9,8},{10,11... | collective-permute-start | bytes 884744 | tf_op jit(solution)/shard_map/ppermute | solution.py:235
  75.1 4.8 %collective-permute-start.3 = (bf16[192,768]{1,0:T(8,128)(2,1)S(1)}, bf16[192,768]{1,0:T(8,128)(2,1)S(1)}, u32[]{:S(2)}, u32[]{:S(2)}) collective-permute-start(bf16[192,768]{1,0:T(8,128)(2,1)S(1)} %collective-permute-done.2.w2_ref), channel_id=1, source_target_pairs={{0,1},{1,0},{2,3},{3,2},{4,5},{5,4},{6,7},{7,6},{8,9},{9,8},{10,11... | collective-permute-start | bytes 884744 | tf_op jit(solution)/shard_map/ppermute | solution.py:235
  108.8 5.0 %collective-permute-start.7 = (bf16[80,384]{1,0:T(8,128)(2,1)S(1)}, bf16[80,384]{1,0:T(8,128)(2,1)S(1)}, u32[]{:S(2)}, u32[]{:S(2)}) collective-permute-start(bf16[80,384]{1,0:T(8,128)(2,1)S(1)} %get-tuple-element.88.own_ref), channel_id=1, source_target_pairs={{0,64},{4,68},{8,72},{12,76},{16,80},{20,84},{24,88},{28,92},{32,9... | collective-permute-start | bytes 184328 | tf_op jit(solution)/shard_map/ppermute | solution.py:287
  115.3 30.7 %copy-start.6 = (bf16[4,80,640]{2,1,0:T(8,128)(2,1)S(1)}, bf16[4,80,640]{2,1,0:T(8,128)(2,1)}, u32[]{:S(2)}) copy-start(bf16[4,80,640]{2,1,0:T(8,128)(2,1)} %get-tuple-element.92.bias0_ref) | copy-start | bytes 1228804
  115.3 29.9 %all-to-all-start.3 = ((bf16[16,2,80,384]{3,2,1,0:T(8,128)(2,1)}), bf16[16,2,80,384]{3,2,1,0:T(8,128)(2,1)S(1)}, u32[]{:S(2)}, u32[]{:S(2)}) async-start(bf16[16,2,80,384]{3,2,1,0:T(8,128)(2,1)} %copy-done.2), calls=%async_computation.3 | async-start | bytes 3932160 | tf_op jit(solution)/shard_map/all_to_all | solution.py:296
  119.3 7.6 %collective-permute-start.9 = (bf16[192,768]{1,0:T(8,128)(2,1)S(1)}, bf16[192,768]{1,0:T(8,128)(2,1)S(1)}, u32[]{:S(2)}, u32[]{:S(2)}) collective-permute-start(bf16[192,768]{1,0:T(8,128)(2,1)S(1)} %get-tuple-element.90.w0_ref), channel_id=1, source_target_pairs={{0,2},{1,3},{2,0},{3,1},{4,6},{5,7},{6,4},{7,5},{8,10},{9,11},{10,... | collective-permute-start | bytes 884744 | tf_op jit(solution)/shard_map/ppermute | solution.py:235
  119.7 25.4 %collective-permute-start.11 = (bf16[4,80,640]{2,1,0:T(8,128)(2,1)}, bf16[4,80,640]{2,1,0:T(8,128)(2,1)S(1)}, u32[]{:S(2)}, u32[]{:S(2)}) collective-permute-start(bf16[4,80,640]{2,1,0:T(8,128)(2,1)} %get-tuple-element.93), channel_id=1, source_target_pairs={{0,1},{1,0},{2,3},{3,2},{4,5},{5,4},{6,7},{7,6},{8,9},{9,8},{10,11... | collective-permute-start | bytes 1228808 | tf_op jit(solution)/shard_map/ppermute | solution.py:235
  121.0 24.2 %collective-permute-start.12 = (bf16[4,80,640]{2,1,0:T(8,128)(2,1)}, bf16[4,80,640]{2,1,0:T(8,128)(2,1)}, u32[]{:S(2)}, u32[]{:S(2)}) collective-permute-start(bf16[4,80,640]{2,1,0:T(8,128)(2,1)} %get-tuple-element.94), channel_id=1, source_target_pairs={{0,2},{1,3},{2,0},{3,1},{4,6},{5,7},{6,4},{7,5},{8,10},{9,11},{10,... | collective-permute-start | bytes 1228808 | tf_op jit(solution)/shard_map/ppermute | solution.py:235
  122.1 23.9 %collective-permute-start.13 = (bf16[4,80,640]{2,1,0:T(8,128)(2,1)}, bf16[4,80,640]{2,1,0:T(8,128)(2,1)}, u32[]{:S(2)}, u32[]{:S(2)}) collective-permute-start(bf16[4,80,640]{2,1,0:T(8,128)(2,1)} %get-tuple-element.95), channel_id=1, source_target_pairs={{0,3},{1,2},{2,1},{3,0},{4,7},{5,6},{6,5},{7,4},{8,11},{9,10},{10,... | collective-permute-start | bytes 1228808 | tf_op jit(solution)/shard_map/ppermute | solution.py:235
  122.6 8.4 %collective-permute-start.8 = (bf16[192,768]{1,0:T(8,128)(2,1)S(1)}, bf16[192,768]{1,0:T(8,128)(2,1)S(1)}, u32[]{:S(2)}, u32[]{:S(2)}) collective-permute-start(bf16[192,768]{1,0:T(8,128)(2,1)S(1)} %get-tuple-element.90.w0_ref), channel_id=1, source_target_pairs={{0,1},{1,0},{2,3},{3,2},{4,5},{5,4},{6,7},{7,6},{8,9},{9,8},{10,11... | collective-permute-start | bytes 884744 | tf_op jit(solution)/shard_map/ppermute | solution.py:235
  126.9 4.8 %collective-permute-start.10 = (bf16[192,768]{1,0:T(8,128)(2,1)S(1)}, bf16[192,768]{1,0:T(8,128)(2,1)S(1)}, u32[]{:S(2)}, u32[]{:S(2)}) collective-permute-start(bf16[192,768]{1,0:T(8,128)(2,1)S(1)} %collective-permute-done.9.w2_ref), channel_id=1, source_target_pairs={{0,1},{1,0},{2,3},{3,2},{4,5},{5,4},{6,7},{7,6},{8,9},{9,8},{10,11... | collective-permute-start | bytes 884744 | tf_op jit(solution)/shard_map/ppermute | solution.py:235
  (25 other events, 161.8 us)
where the time goes:
time: 160 us; the launch traced here: 159 us
  waiting for transfers between devices  45 us (28%)
  blocking collectives  42.2 us (26%)
  starting transfers between devices  34.7 us (22%)
  Pallas kernels  26.1 us (16%)
  local copies, waits for them, and re-layouts  11 us (7%)
    all_to_all x2, waiting for transfers between devices, on_device(): kv = lax.all_to_all(kv, 'row', 0, 0, tiled=True, axis_index_groups=halves)  25.2 us
    all_to_all x1, blocking collectives, exchange(): return lax.all_to_all(x, axis, 0, 0, tiled=True)  17.9 us
    all_gather x2, blocking collectives, on_device(): gated = lax.all_gather(gated, 'col', axis=0, tiled=False)  16.6 us
    ppermute x12, starting transfers between devices, from_step(): return lax.ppermute(x, 'col', [(i, i ^ step) for i in range(NC)])  13.7 us
    all_to_all x1, starting transfers between devices, exchange(): return lax.all_to_all(x, axis, 0, 0, tiled=True)  11.3 us
    unnamed x64, local copies, waits for them, and re-layouts  11 us
    pallas_call x1, Pallas kernels, pair_bias_call(): pl.pallas_call(pair_bias_kernel, grid=(rows // step,), in_specs=[smem(),...  10.3 us
    ppermute x12, waiting for transfers between devices, from_step(): return lax.ppermute(x, 'col', [(i, i ^ step) for i in range(NC)])  10.2 us
  transfers between devices with their start and end apart: 17, of which 9 were waited for; matrix products, arithmetic and copies ran while one was open for 0% of the time, Pallas kernels for 6%

commit v1 on v0

--- a/solution.py
+++ b/solution.py
@@ -17,6 +17,7 @@
 BF = jnp.bfloat16
 F32 = jnp.float32
 VMEM_LIMIT = 16 * 1024 * 1024
+WHOLE_VMEM = 56 * 1024 * 1024
 NT = (((1,), (1,)), ((), ()))
 TN = (((0,), (0,)), ((), ()))
 
@@ -31,11 +32,11 @@
     return centred * lax.rsqrt(spread + EPSILON) * gain_row
 
 
-def call(kernel, out_shape, flops, moved, **kw):
+def call(kernel, out_shape, flops, moved, limit=VMEM_LIMIT, **kw):
     return pl.pallas_call(
         kernel,
         out_shape=out_shape,
-        compiler_params=pltpu.CompilerParams(vmem_limit_bytes=VMEM_LIMIT),
+        compiler_params=pltpu.CompilerParams(vmem_limit_bytes=limit),
         cost_estimate=pl.CostEstimate(flops=flops, bytes_accessed=moved, transcendentals=0),
         **kw,
     )
@@ -72,44 +73,56 @@
         ],
         out_specs=[pl.BlockSpec((own, step, cols), lambda i: (0, i, 0))] * (layers * NC),
         out_shape=[shaped((own, rows, cols), BF)] * (layers * NC),
-        compiler_params=pltpu.CompilerParams(vmem_limit_bytes=56 * 1024 * 1024),
+        compiler_params=pltpu.CompilerParams(vmem_limit_bytes=WHOLE_VMEM),
         cost_estimate=pl.CostEstimate(
             flops=64 * rows * cols * ch, bytes_accessed=2 * rows * cols * (ch + 32), transcendentals=0
         ),
     )(col_at, pair, w_t)
 
 
-def pack_kernel(row_ref, feats_ref, counts_ref, out_ref):
+def pack_kernel(row_ref, feats_ref, gain_ref, w_ref, counts_ref, out_ref):
     rows = out_ref.shape[0]
     tq = counts_ref.shape[1]
+    half = LANES // 2
     last = feats_ref.shape[0] - REACH
+    edges = jnp.concatenate([feats_ref[:REACH], feats_ref[last:]], axis=0).astype(F32)
+    normed = layer_norm(edges, gain_ref[...]).astype(BF)
+    kv = jnp.concatenate([dot(normed, w_ref[1], NT), dot(normed, w_ref[2], NT)], axis=1)
     counts = counts_ref[...].astype(F32)
-    counts = jnp.concatenate([counts, jnp.zeros((1, LANES - tq), F32)], axis=1)
-    top = jnp.where(lax.broadcasted_iota(jnp.int32, (TOP, LANES), 0) == 0, counts, 0.0).astype(BF)
-    head = feats_ref[:REACH]
+    rest = jnp.concatenate([counts[:, half:], jnp.zeros((1, LANES - tq), F32)], axis=1)
+    at = lax.broadcasted_iota(jnp.int32, (TOP, half), 0)
+    counts = jnp.where(at == 0, counts[:, :half], jnp.where(at == 1, rest, 0.0))
+
+    def message(kv):
+        right = jnp.concatenate([kv[2 * TOP :], counts], axis=0)
+        return jnp.concatenate([kv[: 2 * TOP], right], axis=1).astype(BF)
+
+    head = message(kv[:REACH])
     for d in range(rows):
-        out_ref[d, :TOP] = top
-        out_ref[d, TOP:] = head
+        out_ref[d] = head
 
     @pl.when(row_ref[0] + 1 < rows)
     def _():
-        out_ref[row_ref[0] + 1, TOP:] = feats_ref[last:]
+        out_ref[row_ref[0] + 1] = message(kv[REACH:])
 
 
 def atom_kernel(row_ref, msg_ref, feats_ref, gain_ref, w_ref, wab_ref, apair_ref, out_ref, own_ref, counts_ref):
     rows = feats_ref.shape[0]
     n_rows = msg_ref.shape[0]
     tq = out_ref.shape[2]
+    half = LANES // 2
     row = row_ref[0]
     first = row * rows
     total = rows * n_rows
-    prev = msg_ref[jnp.maximum(row - 1, 0), TOP:]
-    nxt = msg_ref[jnp.minimum(row + 1, n_rows - 1), TOP:]
-    x = jnp.concatenate([prev, feats_ref[...], nxt], axis=0).astype(F32)
-    normed = layer_norm(x, gain_ref[...]).astype(BF)
-    q = dot(normed[REACH : REACH + rows], w_ref[0], NT).astype(BF)
-    k = dot(normed, w_ref[1], NT).astype(BF)
-    v = dot(normed, w_ref[2], NT).astype(BF)
+    prev = msg_ref[jnp.maximum(row - 1, 0)].astype(F32)
+    nxt = msg_ref[jnp.minimum(row + 1, n_rows - 1)].astype(F32)
+    normed = layer_norm(feats_ref[...].astype(F32), gain_ref[...]).astype(BF)
+    q = dot(normed, w_ref[0], NT).astype(BF)
+    own = jnp.concatenate([dot(normed, w_ref[1], NT), dot(normed, w_ref[2], NT)], axis=1)
+    kv = jnp.concatenate(
+        [prev[:, :half], prev[:TOP, half:], own, nxt[:, :half], nxt[:TOP, half:]], axis=0
+    ).astype(BF)
+    k, v = kv[:, : half // 2], kv[:, half // 2 :]
     wab = wab_ref[...].astype(F32).T
     bias = apair_ref[0].astype(F32) * wab[0:1, 0:1]
     for c in range(1, apair_ref.shape[0]):
@@ -128,7 +141,11 @@
     )
     out_t = out.T.astype(BF)
 
-    counts = jnp.sum(msg_ref[:, :TOP].astype(F32), axis=1)
+    held = msg_ref[:, TOP:].astype(F32)
+    at = lax.broadcasted_iota(jnp.int32, held.shape, 1)
+    counts = jnp.concatenate(
+        [jnp.sum(jnp.where(at == i, held, 0.0), axis=1)[:, half:] for i in range(2)], axis=1
+    )
     small = counts.astype(BF)
     upto = lax.broadcasted_iota(jnp.int32, (LANES, LANES), 0) <= lax.broadcasted_iota(jnp.int32, (LANES, LANES), 1)
     inside = dot(small, jnp.where(upto, 1.0, 0.0).astype(BF))
@@ -251,14 +268,12 @@
     width = w_attn.shape[3]
     own = heads // NC
 
-    msg = call(pack_kernel, shaped((n_rows, TOP + REACH, LANES), BF), 0, 1 << 19, in_specs=[smem(), vmem(), vmem()], out_specs=vmem())(
-        row_at, atom_feats, atom_counts[None]
-    )
+    w_atom_t = w_atom.transpose(0, 2, 1)
+    msg = call(
+        pack_kernel, shaped((n_rows, 2 * TOP, LANES), BF), 0, 1 << 18, limit=WHOLE_VMEM,
+        in_specs=[smem()] + [vmem()] * 4, out_specs=vmem(),
+    )(row_at, atom_feats, atom_gain[None], w_atom_t, atom_counts[None])
     msg = exchange(msg, "row")
-
-    w_t = w_bias.transpose(0, 2, 1).reshape(layers * heads, ch)
-    local_bias = pair_bias_call(col_at, pair, w_t, layers)
-    msg, *local_bias = lax.optimization_barrier((msg, *local_bias))
 
     head_a = w_atom.shape[2]
     partial, own_counts = call(
@@ -266,11 +281,18 @@
         [shaped((n_rows, head_a, tq), BF), shaped((1, tq), F32)],
         2 * atom_rows * (3 * width_a * head_a + 2 * WK * head_a + head_a * n_rows * tq),
         2 * atom_pair.size,
+        limit=WHOLE_VMEM,
         in_specs=[smem()] + [vmem()] * 6,
         out_specs=[vmem()] * 2,
         scratch_shapes=[pltpu.VMEM((n_rows, LANES), F32)],
-    )(row_at, msg, atom_feats, atom_gain[None], w_atom.transpose(0, 2, 1), w_atom_bias.T, atom_pair)
-    sums = call(sums_kernel, shaped((head_a, tq), BF), 0, 1 << 18)(exchange(partial, "row"))
+    )(row_at, msg, atom_feats, atom_gain[None], w_atom_t, w_atom_bias.T, atom_pair)
+
+    w_t = w_bias.transpose(0, 2, 1).reshape(layers * heads, ch)
+    partial, w_t = lax.optimization_barrier((partial, w_t))
+    parts = exchange(partial, "row")
+    local_bias = pair_bias_call(col_at, pair, w_t, layers)
+    parts, *local_bias = lax.optimization_barrier((parts, *local_bias))
+    sums = call(sums_kernel, shaped((head_a, tq), BF), 0, 1 << 18)(parts)
     sums = lax.all_gather(sums, "col", axis=0, tiled=True)
 
     w_attn_t = w_attn.transpose(0, 1, 3, 2)

time: 160 us -> 157 us (0.981)
  waiting for transfers between devices: 45 us -> 38.6 us
  Pallas kernels: 26.1 us -> 30.3 us
  local copies, waits for them, and re-layouts: 11 us -> 7.74 us
  blocking collectives: 42.2 us -> 44.3 us
    all_to_all x1, starting transfers between devices: 11.3 us -> 4.07 us  [exchange(): return lax.all_to_all(x, axis, 0, 0, tiled=True)]
    ppermute x2, starting transfers between devices: 1.04 us -> 5.7 us  [on_device(): lax.ppermute(kv, 'row', [(i, (i + half) % n_rows) for i in range(n_rows)])]
    ppermute x2, waiting for transfers between devices: 8.88 us -> 4.22 us  [on_device(): lax.ppermute(kv, 'row', [(i, (i + half) % n_rows) for i in range(n_rows)])]
    unnamed x64 -> x52, local copies, waits for them, and re-layouts: 11 us -> 7.7 us
    all_to_all x1, blocking collectives: 17.9 us -> 20.9 us  [exchange(): return lax.all_to_all(x, axis, 0, 0, tiled=True)]
    pallas_call x1, Pallas kernels: 3 us -> 5.86 us  [on_device(): call(atom_kernel, [shaped((n_rows, head_a, tq), BF), shaped((1, tq), F32)...]
    all_to_all x2, waiting for transfers between devices: 25.2 us -> 22.7 us  [on_device(): kv = lax.all_to_all(kv, 'row', 0, 0, tiled=True, axis_index_groups=halves)]
    all_to_all x2, starting transfers between devices: 8.59 us -> 10.8 us  [on_device(): kv = lax.all_to_all(kv, 'row', 0, 0, tiled=True, axis_index_groups=halves)]
  transfers between devices with their start and end apart: 17 -> 17, of which waited for: 9 -> 8; matrix products, arithmetic and copies ran while one was open for 0% -> 0% of each run, Pallas kernels for 6% -> 7%
where the time goes in v1:
time: 157 us
  blocking collectives  44.3 us (28%)
  waiting for transfers between devices  38.6 us (25%)
  starting transfers between devices  35.4 us (23%)
  Pallas kernels  30.3 us (19%)
  local copies, waits for them, and re-layouts  7.74 us (5%)
    all_to_all x2, waiting for transfers between devices, on_device(): kv = lax.all_to_all(kv, 'row', 0, 0, tiled=True, axis_index_groups=halves)  22.7 us
    all_to_all x1, blocking collectives, exchange(): return lax.all_to_all(x, axis, 0, 0, tiled=True)  20.9 us
    all_gather x2, blocking collectives, on_device(): gated = lax.all_gather(gated, 'col', axis=0, tiled=False)  16.2 us
    ppermute x12, starting transfers between devices, from_step(): return lax.ppermute(x, 'col', [(i, i ^ step) for i in range(NC)])  14.8 us
    ppermute x12, waiting for transfers between devices, from_step(): return lax.ppermute(x, 'col', [(i, i ^ step) for i in range(NC)])  11.6 us
    all_to_all x2, starting transfers between devices, on_device(): kv = lax.all_to_all(kv, 'row', 0, 0, tiled=True, axis_index_groups=halves)  10.8 us
    pallas_call x1, Pallas kernels, pair_bias_call(): pl.pallas_call(pair_bias_kernel, grid=(rows // step,), in_specs=[smem(),...  10.4 us
    pallas_call x2, Pallas kernels, on_device(): call(attend_kernel, shaped((tq, width), BF), 4 * tq * n_rows * tq * width...  8.72 us
  transfers between devices with their start and end apart: 17, of which 8 were waited for; matrix products, arithmetic and copies ran while one was open for 0% of the time, Pallas kernels for 7%

profile of v1, /device:TPU:1, one launch (start us, length us, event | category | flops | bytes accessed | tf_op | source)
XLA Modules:
  0.0 156.5 jit_solution(6574209513031700680)
XLA Ops:
  0.0 2.1 %shard_map.127 = bf16[32,32,128]{2,1,0:T(8,128)(2,1)} custom-call(s32[1]{0:T(128)} %bitcast.1.row_ref, bf16[640,128]{1,0:T(8,128)(2,1)} %feats_ref.3, f32[1,128]{1,0:T(1,128)} %bitcast.23, bf16[3,32,128]{2,1,0:T(8,128)(2,1)} %bitcast.20, s32[1,80]{1,0:T(1,128)} %bitcast.26), custom_call_target="tpu_custom_call" | custom-call | bytes 262144 | tf_op jit(solution)/shard_map/pallas_call | solution.py:272
  2.1 20.9 %all_to_all.20.msg_ref = bf16[32,32,128]{2,1,0:T(8,128)(2,1)} all-to-all(bf16[32,32,128]{2,1,0:T(8,128)(2,1)} %shard_map.127), channel_id=1, replica_groups=mesh['row'=32,'col'=4] {'row'}, dimensions={0} | all-to-all | bytes 524288 | tf_op jit(solution)/shard_map/all_to_all | solution.py:248
  23.1 5.9 %shard_map.128 = (bf16[32,32,80]{2,1,0:T(8,128)(2,1)}, f32[1,80]{1,0:T(1,128)}) custom-call(s32[1]{0:T(128)} %bitcast.1.row_ref, bf16[32,32,128]{2,1,0:T(8,128)(2,1)} %all_to_all.20.msg_ref, bf16[640,128]{1,0:T(8,128)(2,1)} %feats_ref.3, f32[1,128]{1,0:T(1,128)} %bitcast.24, bf16[3,32,128]{2,1,0:T(8,128)(2,1)} %bitcast.21, bf16[1,16]{1,0:T(2,128)(2,1)} %bitcast.25, ...), custom_call_target="tpu_custom_call" | custom-call | flops 131072000 | bytes 2621440 | tf_op jit(solution)/shard_map/pallas_call | solution.py:279
  28.9 4.1 %all-to-all-start.1 = ((bf16[32,32,80]{2,1,0:T(8,128)(2,1)}), bf16[32,32,80]{2,1,0:T(8,128)(2,1)S(1)}, u32[]{:S(2)}, u32[]{:S(2)}) async-start(bf16[32,32,80]{2,1,0:T(8,128)(2,1)} %get-tuple-element.55), calls=%async_computation.1 | async-start | bytes 524288 | tf_op jit(solution)/shard_map/all_to_all | solution.py:248
  33.1 10.4 %shard_map.129 = (bf16[4,80,640]{2,1,0:T(8,128)(2,1)}, bf16[4,80,640]{2,1,0:T(8,128)(2,1)}, bf16[4,80,640]{2,1,0:T(8,128)(2,1)}, bf16[4,80,640]{2,1,0:T(8,128)(2...) custom-call(s32[1]{0:T(128)} %bitcast.col_ref, ...), custom_call_target="tpu_custom_call" | custom-call | flops 419430400 | bytes 16384000 | tf_op jit(solution)/shard_map/pallas_call | solution.py:66
  43.6 7.2 %all_gather.15.sums_ref = bf16[128,80]{1,0:T(8,128)(2,1)S(1)} all-gather(bf16[32,80]{1,0:T(8,128)(2,1)S(1)} %shard_map.130), channel_id=1, replica_groups=mesh['row'=32,'col'=4] {'col'}, dimensions={0}, use_global_device_ids=true | all-gather | bytes 25600 | tf_op jit(solution)/shard_map/all_gather | solution.py:296
  51.6 2.9 %collective-permute-start = (bf16[80,384]{1,0:T(8,128)(2,1)S(1)}, bf16[80,384]{1,0:T(8,128)(2,1)S(1)}, u32[]{:S(2)}, u32[]{:S(2)}) collective-permute-start(bf16[80,384]{1,0:T(8,128)(2,1)S(1)} %get-tuple-element.74.own_ref), channel_id=1, source_target_pairs={{0,64},{4,68},{8,72},{12,76},{16,80},{20,84},{24,88},{28,92},{32,9... | collective-permute-start | bytes 184328 | tf_op jit(solution)/shard_map/ppermute | solution.py:309
  54.6 2.0 %collective-permute-done.far_ref = bf16[80,384]{1,0:T(8,128)(2,1)S(1)} collective-permute-done((bf16[80,384]{1,0:T(8,128)(2,1)S(1)}, bf16[80,384]{1,0:T(8,128)(2,1)S(1)}, u32[]{:S(2)}, u32[]{:S(2)}) %collective-permute-start) | collective-permute-done | bytes 61472 | tf_op jit(solution)/shard_map/ppermute | solution.py:309
  58.1 6.8 %all-to-all-start.2 = ((bf16[16,2,80,384]{3,2,1,0:T(8,128)(2,1)}), bf16[16,2,80,384]{3,2,1,0:T(8,128)(2,1)}, u32[]{:S(2)}, u32[]{:S(2)}) async-start(bf16[16,2,80,384]{3,2,1,0:T(8,128)(2,1)} %copy-done.1), calls=%async_computation.2 | async-start | bytes 3932160 | tf_op jit(solution)/shard_map/all_to_all | solution.py:318
  68.7 3.6 %collective-permute-done.2.w2_ref = bf16[192,768]{1,0:T(8,128)(2,1)S(1)} collective-permute-done((bf16[192,768]{1,0:T(8,128)(2,1)S(1)}, bf16[192,768]{1,0:T(8,128)(2,1)S(1)}, u32[]{:S(2)}, u32[]{:S(2)}) %collective-permute-start.2) | collective-permute-done | bytes 294944 | tf_op jit(solution)/shard_map/ppermute | solution.py:252
  72.3 3.9 %collective-permute-start.3 = (bf16[192,768]{1,0:T(8,128)(2,1)S(1)}, bf16[192,768]{1,0:T(8,128)(2,1)S(1)}, u32[]{:S(2)}, u32[]{:S(2)}) collective-permute-start(bf16[192,768]{1,0:T(8,128)(2,1)S(1)} %collective-permute-done.2.w2_ref), channel_id=1, source_target_pairs={{0,1},{1,0},{2,3},{3,2},{4,5},{5,4},{6,7},{7,6},{8,9},{9,8},{10,11... | collective-permute-start | bytes 884744 | tf_op jit(solution)/shard_map/ppermute | solution.py:252
  78.4 10.9 %all-to-all-done.2.kv_ref = bf16[16,2,80,384]{3,2,1,0:T(8,128)(2,1)} async-done(((bf16[16,2,80,384]{3,2,1,0:T(8,128)(2,1)}), bf16[16,2,80,384]{3,2,1,0:T(8,128)(2,1)}, u32[]{:S(2)}, u32[]{:S(2)}) %all-to-all-start.2) | async-done | bytes 1966112 | tf_op jit(solution)/shard_map/all_to_all | solution.py:318
  89.3 2.4 %collective-permute-done.6.bias3_ref = bf16[4,80,640]{2,1,0:T(8,128)(2,1)} collective-permute-done((bf16[4,80,640]{2,1,0:T(8,128)(2,1)}, bf16[4,80,640]{2,1,0:T(8,128)(2,1)}, u32[]{:S(2)}, u32[]{:S(2)}) %collective-permute-start.6) | collective-permute-done | bytes 409632 | tf_op jit(solution)/shard_map/ppermute | solution.py:252
  91.7 4.7 %shard_map.133 = bf16[80,192]{1,0:T(8,128)(2,1)S(1)} custom-call(s32[1]{0:T(128)} %bitcast.col_ref, s32[1]{0:T(128)S(6)} %select_n.5.half_ref, bf16[2,80,192]{2,1,0:T(8,128)(2,1)S(1)} %get-tuple-element.68.qg_ref, bf16[16,2,80,384]{3,2,1,0:T(8,128)(2,1)} %all-to-all-done.2.kv_ref, bf16[4,80,640]{2,1,0:T(8,128)(2,1)S(1)} %copy-done.4, ...), custom_call_target="tpu_custom_call" | custom-call | flops 157286400 | bytes 1638400 | tf_op jit(solution)/shard_map/pallas_call | solution.py:321
  96.4 8.0 %all-gather = bf16[320,192]{1,0:T(8,128)(2,1)S(1)} all-gather(bf16[80,192]{1,0:T(8,128)(2,1)S(1)} %shard_map.133), channel_id=2, replica_groups=mesh['row'=32,'col'=4] {'col'}, dimensions={0}, use_global_device_ids=true | all-gather | bytes 153600 | tf_op jit(solution)/shard_map/all_gather | solution.py:325
  106.2 2.8 %collective-permute-start.7 = (bf16[80,384]{1,0:T(8,128)(2,1)S(1)}, bf16[80,384]{1,0:T(8,128)(2,1)S(1)}, u32[]{:S(2)}, u32[]{:S(2)}) collective-permute-start(bf16[80,384]{1,0:T(8,128)(2,1)S(1)} %get-tuple-element.92.own_ref), channel_id=1, source_target_pairs={{0,64},{4,68},{8,72},{12,76},{16,80},{20,84},{24,88},{28,92},{32,9... | collective-permute-start | bytes 184328 | tf_op jit(solution)/shard_map/ppermute | solution.py:309
  108.9 2.2 %collective-permute-done.7.far_ref = bf16[80,384]{1,0:T(8,128)(2,1)S(1)} collective-permute-done((bf16[80,384]{1,0:T(8,128)(2,1)S(1)}, bf16[80,384]{1,0:T(8,128)(2,1)S(1)}, u32[]{:S(2)}, u32[]{:S(2)}) %collective-permute-start.7) | collective-permute-done | bytes 61472 | tf_op jit(solution)/shard_map/ppermute | solution.py:309
  112.6 4.0 %all-to-all-start.3 = ((bf16[16,2,80,384]{3,2,1,0:T(8,128)(2,1)}), bf16[16,2,80,384]{3,2,1,0:T(8,128)(2,1)S(1)}, u32[]{:S(2)}, u32[]{:S(2)}) async-start(bf16[16,2,80,384]{3,2,1,0:T(8,128)(2,1)} %copy-done.2), calls=%async_computation.3 | async-start | bytes 3932160 | tf_op jit(solution)/shard_map/all_to_all | solution.py:318
  120.3 4.0 %collective-permute-done.9.w2_ref = bf16[192,768]{1,0:T(8,128)(2,1)S(1)} collective-permute-done((bf16[192,768]{1,0:T(8,128)(2,1)S(1)}, bf16[192,768]{1,0:T(8,128)(2,1)S(1)}, u32[]{:S(2)}, u32[]{:S(2)}) %collective-permute-start.9) | collective-permute-done | bytes 294944 | tf_op jit(solution)/shard_map/ppermute | solution.py:252
  124.2 3.5 %collective-permute-start.10 = (bf16[192,768]{1,0:T(8,128)(2,1)S(1)}, bf16[192,768]{1,0:T(8,128)(2,1)S(1)}, u32[]{:S(2)}, u32[]{:S(2)}) collective-permute-start(bf16[192,768]{1,0:T(8,128)(2,1)S(1)} %collective-permute-done.9.w2_ref), channel_id=1, source_target_pairs={{0,1},{1,0},{2,3},{3,2},{4,5},{5,4},{6,7},{7,6},{8,9},{9,8},{10,11... | collective-permute-start | bytes 884744 | tf_op jit(solution)/shard_map/ppermute | solution.py:252
  129.9 11.8 %all-to-all-done.3.kv_ref = bf16[16,2,80,384]{3,2,1,0:T(8,128)(2,1)S(1)} async-done(((bf16[16,2,80,384]{3,2,1,0:T(8,128)(2,1)}), bf16[16,2,80,384]{3,2,1,0:T(8,128)(2,1)S(1)}, u32[]{:S(2)}, u32[]{:S(2)}) %all-to-all-start.3) | async-done | bytes 1966112 | tf_op jit(solution)/shard_map/all_to_all | solution.py:318
  141.7 1.6 %collective-permute-done.13.bias3_ref = bf16[4,80,640]{2,1,0:T(8,128)(2,1)} collective-permute-done((bf16[4,80,640]{2,1,0:T(8,128)(2,1)}, bf16[4,80,640]{2,1,0:T(8,128)(2,1)}, u32[]{:S(2)}, u32[]{:S(2)}) %collective-permute-start.13) | collective-permute-done | bytes 409632 | tf_op jit(solution)/shard_map/ppermute | solution.py:252
  143.4 4.0 %shard_map.136 = bf16[80,192]{1,0:T(8,128)(2,1)S(1)} custom-call(s32[1]{0:T(128)} %bitcast.col_ref, s32[1]{0:T(128)S(6)} %select_n.5.half_ref, bf16[2,80,192]{2,1,0:T(8,128)(2,1)S(1)} %get-tuple-element.86.qg_ref, bf16[16,2,80,384]{3,2,1,0:T(8,128)(2,1)S(1)} %all-to-all-done.3.kv_ref, bf16[4,80,640]{2,1,0:T(8,128)(2,1)S(1)} %copy-done.3, ...), custom_call_target="tpu_custom_call" | custom-call | flops 157286400 | bytes 1638400 | tf_op jit(solution)/shard_map/pallas_call | solution.py:321
  147.4 8.2 %all-gather.1 = bf16[320,192]{1,0:T(8,128)(2,1)S(1)} all-gather(bf16[80,192]{1,0:T(8,128)(2,1)S(1)} %shard_map.136), channel_id=3, replica_groups=mesh['row'=32,'col'=4] {'col'}, dimensions={0}, use_global_device_ids=true | all-gather | bytes 153600 | tf_op jit(solution)/shard_map/all_gather | solution.py:325
  (78 shorter events, 18.3 us)
Async XLA Ops:
  28.9 14.6 %all-to-all-start.1 = ((bf16[32,32,80]{2,1,0:T(8,128)(2,1)}), bf16[32,32,80]{2,1,0:T(8,128)(2,1)S(1)}, u32[]{:S(2)}, u32[]{:S(2)}) async-start(bf16[32,32,80]{2,1,0:T(8,128)(2,1)} %get-tuple-element.55), calls=%async_computation.1 | async-start | bytes 524288 | tf_op jit(solution)/shard_map/all_to_all | solution.py:248
  33.0 17.7 %copy-start = (bf16[2,4,768,192]{2,3,1,0:T(8,128)(2,1)S(1)}, bf16[2,4,768,192]{2,3,1,0:T(8,128)(2,1)}, u32[]{:S(2)}) copy-start(bf16[2,4,768,192]{2,3,1,0:T(8,128)(2,1)} %param.22) | copy-start | bytes 7077892
  33.0 17.7 %copy-start.21 = (bf16[128,768]{1,0:T(8,128)(2,1)S(1)}, bf16[128,768]{1,0:T(8,128)(2,1)}, u32[]{:S(2)}) copy-start(bf16[128,768]{1,0:T(8,128)(2,1)} %w_pool_ref.1) | copy-start | bytes 589828
  33.1 17.7 %copy-start.22 = (bf16[80,768]{1,0:T(8,128)(2,1)S(1)}, bf16[80,768]{1,0:T(8,128)(2,1)}, u32[]{:S(2)}) copy-start(bf16[80,768]{1,0:T(8,128)(2,1)} %single_ref.1) | copy-start | bytes 368644
  33.1 17.7 %copy-start.23 = (f32[2,768]{1,0:T(2,128)S(1)}, f32[2,768]{1,0:T(2,128)}, u32[]{:S(2)}) copy-start(f32[2,768]{1,0:T(2,128)} %gain_ref.3) | copy-start | bytes 18436
  33.1 17.7 %copy-start.24 = (f32[1,80]{1,0:T(1,128)S(1)}, f32[1,80]{1,0:T(1,128)}, u32[]{:S(2)}) copy-start(f32[1,80]{1,0:T(1,128)} %get-tuple-element.66.counts_ref) | copy-start | bytes 964
  51.6 5.0 %collective-permute-start = (bf16[80,384]{1,0:T(8,128)(2,1)S(1)}, bf16[80,384]{1,0:T(8,128)(2,1)S(1)}, u32[]{:S(2)}, u32[]{:S(2)}) collective-permute-start(bf16[80,384]{1,0:T(8,128)(2,1)S(1)} %get-tuple-element.74.own_ref), channel_id=1, source_target_pairs={{0,64},{4,68},{8,72},{12,76},{16,80},{20,84},{24,88},{28,92},{32,9... | collective-permute-start | bytes 184328 | tf_op jit(solution)/shard_map/ppermute | solution.py:309
  58.1 33.6 %copy-start.4 = (bf16[4,80,640]{2,1,0:T(8,128)(2,1)S(1)}, bf16[4,80,640]{2,1,0:T(8,128)(2,1)}, u32[]{:S(2)}) copy-start(bf16[4,80,640]{2,1,0:T(8,128)(2,1)} %get-tuple-element.78.bias0_ref) | copy-start | bytes 1228804
  58.1 31.2 %all-to-all-start.2 = ((bf16[16,2,80,384]{3,2,1,0:T(8,128)(2,1)}), bf16[16,2,80,384]{3,2,1,0:T(8,128)(2,1)}, u32[]{:S(2)}, u32[]{:S(2)}) async-start(bf16[16,2,80,384]{3,2,1,0:T(8,128)(2,1)} %copy-done.1), calls=%async_computation.2 | async-start | bytes 3932160 | tf_op jit(solution)/shard_map/all_to_all | solution.py:318
  64.9 7.4 %collective-permute-start.2 = (bf16[192,768]{1,0:T(8,128)(2,1)S(1)}, bf16[192,768]{1,0:T(8,128)(2,1)S(1)}, u32[]{:S(2)}, u32[]{:S(2)}) collective-permute-start(bf16[192,768]{1,0:T(8,128)(2,1)S(1)} %get-tuple-element.76.w0_ref), channel_id=1, source_target_pairs={{0,2},{1,3},{2,0},{3,1},{4,6},{5,7},{6,4},{7,5},{8,10},{9,11},{10,... | collective-permute-start | bytes 884744 | tf_op jit(solution)/shard_map/ppermute | solution.py:252
  65.3 23.9 %collective-permute-start.4 = (bf16[4,80,640]{2,1,0:T(8,128)(2,1)}, bf16[4,80,640]{2,1,0:T(8,128)(2,1)}, u32[]{:S(2)}, u32[]{:S(2)}) collective-permute-start(bf16[4,80,640]{2,1,0:T(8,128)(2,1)} %get-tuple-element.79), channel_id=1, source_target_pairs={{0,1},{1,0},{2,3},{3,2},{4,5},{5,4},{6,7},{7,6},{8,9},{9,8},{10,11... | collective-permute-start | bytes 1228808 | tf_op jit(solution)/shard_map/ppermute | solution.py:252
  66.9 22.4 %collective-permute-start.5 = (bf16[4,80,640]{2,1,0:T(8,128)(2,1)}, bf16[4,80,640]{2,1,0:T(8,128)(2,1)}, u32[]{:S(2)}, u32[]{:S(2)}) collective-permute-start(bf16[4,80,640]{2,1,0:T(8,128)(2,1)} %get-tuple-element.80), channel_id=1, source_target_pairs={{0,2},{1,3},{2,0},{3,1},{4,6},{5,7},{6,4},{7,5},{8,10},{9,11},{10,... | collective-permute-start | bytes 1228808 | tf_op jit(solution)/shard_map/ppermute | solution.py:252
  68.0 23.7 %collective-permute-start.6 = (bf16[4,80,640]{2,1,0:T(8,128)(2,1)}, bf16[4,80,640]{2,1,0:T(8,128)(2,1)}, u32[]{:S(2)}, u32[]{:S(2)}) collective-permute-start(bf16[4,80,640]{2,1,0:T(8,128)(2,1)} %get-tuple-element.81), channel_id=1, source_target_pairs={{0,3},{1,2},{2,1},{3,0},{4,7},{5,6},{6,5},{7,4},{8,11},{9,10},{10,... | collective-permute-start | bytes 1228808 | tf_op jit(solution)/shard_map/ppermute | solution.py:252
  68.5 8.4 %collective-permute-start.1 = (bf16[192,768]{1,0:T(8,128)(2,1)S(1)}, bf16[192,768]{1,0:T(8,128)(2,1)S(1)}, u32[]{:S(2)}, u32[]{:S(2)}) collective-permute-start(bf16[192,768]{1,0:T(8,128)(2,1)S(1)} %get-tuple-element.76.w0_ref), channel_id=1, source_target_pairs={{0,1},{1,0},{2,3},{3,2},{4,5},{5,4},{6,7},{7,6},{8,9},{9,8},{10,11... | collective-permute-start | bytes 884744 | tf_op jit(solution)/shard_map/ppermute | solution.py:252
  72.3 5.3 %collective-permute-start.3 = (bf16[192,768]{1,0:T(8,128)(2,1)S(1)}, bf16[192,768]{1,0:T(8,128)(2,1)S(1)}, u32[]{:S(2)}, u32[]{:S(2)}) collective-permute-start(bf16[192,768]{1,0:T(8,128)(2,1)S(1)} %collective-permute-done.2.w2_ref), channel_id=1, source_target_pairs={{0,1},{1,0},{2,3},{3,2},{4,5},{5,4},{6,7},{7,6},{8,9},{9,8},{10,11... | collective-permute-start | bytes 884744 | tf_op jit(solution)/shard_map/ppermute | solution.py:252
  106.2 5.0 %collective-permute-start.7 = (bf16[80,384]{1,0:T(8,128)(2,1)S(1)}, bf16[80,384]{1,0:T(8,128)(2,1)S(1)}, u32[]{:S(2)}, u32[]{:S(2)}) collective-permute-start(bf16[80,384]{1,0:T(8,128)(2,1)S(1)} %get-tuple-element.92.own_ref), channel_id=1, source_target_pairs={{0,64},{4,68},{8,72},{12,76},{16,80},{20,84},{24,88},{28,92},{32,9... | collective-permute-start | bytes 184328 | tf_op jit(solution)/shard_map/ppermute | solution.py:309
  112.6 30.7 %copy-start.3 = (bf16[4,80,640]{2,1,0:T(8,128)(2,1)S(1)}, bf16[4,80,640]{2,1,0:T(8,128)(2,1)}, u32[]{:S(2)}) copy-start(bf16[4,80,640]{2,1,0:T(8,128)(2,1)} %get-tuple-element.96.bias0_ref) | copy-start | bytes 1228804
  112.6 29.1 %all-to-all-start.3 = ((bf16[16,2,80,384]{3,2,1,0:T(8,128)(2,1)}), bf16[16,2,80,384]{3,2,1,0:T(8,128)(2,1)S(1)}, u32[]{:S(2)}, u32[]{:S(2)}) async-start(bf16[16,2,80,384]{3,2,1,0:T(8,128)(2,1)} %copy-done.2), calls=%async_computation.3 | async-start | bytes 3932160 | tf_op jit(solution)/shard_map/all_to_all | solution.py:318
  116.7 7.6 %collective-permute-start.9 = (bf16[192,768]{1,0:T(8,128)(2,1)S(1)}, bf16[192,768]{1,0:T(8,128)(2,1)S(1)}, u32[]{:S(2)}, u32[]{:S(2)}) collective-permute-start(bf16[192,768]{1,0:T(8,128)(2,1)S(1)} %get-tuple-element.94.w0_ref), channel_id=1, source_target_pairs={{0,2},{1,3},{2,0},{3,1},{4,6},{5,7},{6,4},{7,5},{8,10},{9,11},{10,... | collective-permute-start | bytes 884744 | tf_op jit(solution)/shard_map/ppermute | solution.py:252
  117.1 24.6 %collective-permute-start.11 = (bf16[4,80,640]{2,1,0:T(8,128)(2,1)}, bf16[4,80,640]{2,1,0:T(8,128)(2,1)S(1)}, u32[]{:S(2)}, u32[]{:S(2)}) collective-permute-start(bf16[4,80,640]{2,1,0:T(8,128)(2,1)} %get-tuple-element.97), channel_id=1, source_target_pairs={{0,1},{1,0},{2,3},{3,2},{4,5},{5,4},{6,7},{7,6},{8,9},{9,8},{10,11... | collective-permute-start | bytes 1228808 | tf_op jit(solution)/shard_map/ppermute | solution.py:252
  118.4 23.3 %collective-permute-start.12 = (bf16[4,80,640]{2,1,0:T(8,128)(2,1)}, bf16[4,80,640]{2,1,0:T(8,128)(2,1)}, u32[]{:S(2)}, u32[]{:S(2)}) collective-permute-start(bf16[4,80,640]{2,1,0:T(8,128)(2,1)} %get-tuple-element.98), channel_id=1, source_target_pairs={{0,2},{1,3},{2,0},{3,1},{4,6},{5,7},{6,4},{7,5},{8,10},{9,11},{10,... | collective-permute-start | bytes 1228808 | tf_op jit(solution)/shard_map/ppermute | solution.py:252
  119.5 23.8 %collective-permute-start.13 = (bf16[4,80,640]{2,1,0:T(8,128)(2,1)}, bf16[4,80,640]{2,1,0:T(8,128)(2,1)}, u32[]{:S(2)}, u32[]{:S(2)}) collective-permute-start(bf16[4,80,640]{2,1,0:T(8,128)(2,1)} %get-tuple-element.99), channel_id=1, source_target_pairs={{0,3},{1,2},{2,1},{3,0},{4,7},{5,6},{6,5},{7,4},{8,11},{9,10},{10,... | collective-permute-start | bytes 1228808 | tf_op jit(solution)/shard_map/ppermute | solution.py:252
  120.0 8.4 %collective-permute-start.8 = (bf16[192,768]{1,0:T(8,128)(2,1)S(1)}, bf16[192,768]{1,0:T(8,128)(2,1)S(1)}, u32[]{:S(2)}, u32[]{:S(2)}) collective-permute-start(bf16[192,768]{1,0:T(8,128)(2,1)S(1)} %get-tuple-element.94.w0_ref), channel_id=1, source_target_pairs={{0,1},{1,0},{2,3},{3,2},{4,5},{5,4},{6,7},{7,6},{8,9},{9,8},{10,11... | collective-permute-start | bytes 884744 | tf_op jit(solution)/shard_map/ppermute | solution.py:252
  124.2 4.9 %collective-permute-start.10 = (bf16[192,768]{1,0:T(8,128)(2,1)S(1)}, bf16[192,768]{1,0:T(8,128)(2,1)S(1)}, u32[]{:S(2)}, u32[]{:S(2)}) collective-permute-start(bf16[192,768]{1,0:T(8,128)(2,1)S(1)} %collective-permute-done.9.w2_ref), channel_id=1, source_target_pairs={{0,1},{1,0},{2,3},{3,2},{4,5},{5,4},{6,7},{7,6},{8,9},{9,8},{10,11... | collective-permute-start | bytes 884744 | tf_op jit(solution)/shard_map/ppermute | solution.py:252
  (19 other events, 123.6 us)

commit v2 on v1

--- a/solution.py
+++ b/solution.py
@@ -106,8 +106,19 @@
         out_ref[row_ref[0] + 1] = message(kv[REACH:])
 
 
-def atom_kernel(row_ref, msg_ref, feats_ref, gain_ref, w_ref, wab_ref, apair_ref, out_ref, own_ref, counts_ref):
-    rows = feats_ref.shape[0]
+def atom_own_kernel(feats_ref, gain_ref, w_ref, wab_ref, apair_ref, q_ref, kv_ref, bias_ref):
+    normed = layer_norm(feats_ref[...].astype(F32), gain_ref[...]).astype(BF)
+    q_ref[...] = dot(normed, w_ref[0], NT).astype(BF)
+    kv_ref[...] = jnp.concatenate([dot(normed, w_ref[1], NT), dot(normed, w_ref[2], NT)], axis=1).astype(BF)
+    wab = wab_ref[...].astype(F32).T
+    bias = apair_ref[0].astype(F32) * wab[0:1, 0:1]
+    for c in range(1, apair_ref.shape[0]):
+        bias += apair_ref[c].astype(F32) * wab[c : c + 1, 0:1]
+    bias_ref[...] = bias
+
+
+def atom_kernel(row_ref, msg_ref, q_ref, kv_ref, bias_ref, out_ref, own_ref, counts_ref):
+    rows = q_ref.shape[0]
     n_rows = msg_ref.shape[0]
     tq = out_ref.shape[2]
     half = LANES // 2
@@ -116,17 +127,11 @@
     total = rows * n_rows
     prev = msg_ref[jnp.maximum(row - 1, 0)].astype(F32)
     nxt = msg_ref[jnp.minimum(row + 1, n_rows - 1)].astype(F32)
-    normed = layer_norm(feats_ref[...].astype(F32), gain_ref[...]).astype(BF)
-    q = dot(normed, w_ref[0], NT).astype(BF)
-    own = jnp.concatenate([dot(normed, w_ref[1], NT), dot(normed, w_ref[2], NT)], axis=1)
+    q, bias = q_ref[...], bias_ref[...]
     kv = jnp.concatenate(
-        [prev[:, :half], prev[:TOP, half:], own, nxt[:, :half], nxt[:TOP, half:]], axis=0
+        [prev[:, :half], prev[:TOP, half:], kv_ref[...].astype(F32), nxt[:, :half], nxt[:TOP, half:]], axis=0
     ).astype(BF)
     k, v = kv[:, : half // 2], kv[:, half // 2 :]
-    wab = wab_ref[...].astype(F32).T
-    bias = apair_ref[0].astype(F32) * wab[0:1, 0:1]
-    for c in range(1, apair_ref.shape[0]):
-        bias += apair_ref[c].astype(F32) * wab[c : c + 1, 0:1]
     scores = jnp.concatenate(
         [dot(q[at : at + QBLOCK], k[at : at + WK], NT) for at in range(0, rows, QBLOCK)], axis=0
     )
@@ -276,16 +281,20 @@
     msg = exchange(msg, "row")
 
     head_a = w_atom.shape[2]
+    own_atoms = call(
+        atom_own_kernel,
+        [shaped((atom_rows, head_a), BF), shaped((atom_rows, 2 * head_a), BF), shaped((atom_rows, WK), F32)],
+        2 * atom_rows * 3 * width_a * head_a, 2 * atom_pair.size, limit=WHOLE_VMEM,
+        in_specs=[vmem()] * 5, out_specs=[vmem()] * 3,
+    )(atom_feats, atom_gain[None], w_atom_t, w_atom_bias.T, atom_pair)
     partial, own_counts = call(
         atom_kernel,
         [shaped((n_rows, head_a, tq), BF), shaped((1, tq), F32)],
-        2 * atom_rows * (3 * width_a * head_a + 2 * WK * head_a + head_a * n_rows * tq),
-        2 * atom_pair.size,
-        limit=WHOLE_VMEM,
-        in_specs=[smem()] + [vmem()] * 6,
+        2 * atom_rows * (2 * WK * head_a + head_a * n_rows * tq), 1 << 20, limit=WHOLE_VMEM,
+        in_specs=[smem()] + [vmem()] * 4,
         out_specs=[vmem()] * 2,
         scratch_shapes=[pltpu.VMEM((n_rows, LANES), F32)],
-    )(row_at, msg, atom_feats, atom_gain[None], w_atom_t, w_atom_bias.T, atom_pair)
+    )(row_at, msg, *own_atoms)
 
     w_t = w_bias.transpose(0, 2, 1).reshape(layers * heads, ch)
     partial, w_t = lax.optimization_barrier((partial, w_t))

time: 157 us -> 156 us (level)
  blocking collectives: 44.3 us -> 23.2 us
  starting transfers between devices: 35.4 us -> 47.1 us
  waiting for transfers between devices: 38.6 us -> 43.7 us
  Pallas kernels: 30.3 us -> 32.7 us
    all_to_all x1 -> x0, blocking collectives: 20.9 us -> none  [exchange(): return lax.all_to_all(x, axis, 0, 0, tiled=True)]
    all_to_all x1 -> x2, starting transfers between devices: 4.07 us -> 15.4 us  [exchange(): return lax.all_to_all(x, axis, 0, 0, tiled=True)]
    all_to_all x1 -> x2, waiting for transfers between devices: 0.01 us -> 5.65 us  [exchange(): return lax.all_to_all(x, axis, 0, 0, tiled=True)]
    pallas_call x0 -> x1, Pallas kernels: none -> 3.85 us  [on_device(): call(atom_own_kernel, [shaped((atom_rows, head_a), BF), shaped((atom_rows...]
    unnamed x52 -> x54, local copies, waits for them, and re-layouts: 7.7 us -> 8.38 us
  transfers between devices with their start and end apart: 17 -> 18, of which waited for: 8 -> 9; matrix products, arithmetic and copies ran while one was open for 0% -> 0% of each run, Pallas kernels for 7% -> 9%
where the time goes in v2:
time: 156 us; the launch traced here: 155 us
  starting transfers between devices  47.1 us (30%)
  waiting for transfers between devices  43.7 us (28%)
  Pallas kernels  32.7 us (21%)
  blocking collectives  23.2 us (15%)
  local copies, waits for them, and re-layouts  8.42 us (5%)
    all_to_all x2, waiting for transfers between devices, on_device(): kv = lax.all_to_all(kv, 'row', 0, 0, tiled=True, axis_index_groups=halves)  21.9 us
    all_gather x2, blocking collectives, on_device(): gated = lax.all_gather(gated, 'col', axis=0, tiled=False)  16.1 us
    all_to_all x2, starting transfers between devices, exchange(): return lax.all_to_all(x, axis, 0, 0, tiled=True)  15.4 us
    ppermute x12, starting transfers between devices, from_step(): return lax.ppermute(x, 'col', [(i, i ^ step) for i in range(NC)])  15.3 us
    ppermute x12, waiting for transfers between devices, from_step(): return lax.ppermute(x, 'col', [(i, i ^ step) for i in range(NC)])  12 us
    all_to_all x2, starting transfers between devices, on_device(): kv = lax.all_to_all(kv, 'row', 0, 0, tiled=True, axis_index_groups=halves)  10.7 us
    pallas_call x1, Pallas kernels, pair_bias_call(): pl.pallas_call(pair_bias_kernel, grid=(rows // step,), in_specs=[smem(),...  10.4 us
    pallas_call x2, Pallas kernels, on_device(): call(attend_kernel, shaped((tq, width), BF), 4 * tq * n_rows * tq * width...  8.72 us
  transfers between devices with their start and end apart: 18, of which 9 were waited for; matrix products, arithmetic and copies ran while one was open for 0% of the time, Pallas kernels for 9%

profile of v2, /device:TPU:1, one launch (start us, length us, event | category | flops | bytes accessed | tf_op | source)
XLA Modules:
  0.0 155.4 jit_solution(1682120943512623738)
XLA Ops:
  2.1 11.3 %all-to-all-start = ((bf16[32,32,128]{2,1,0:T(8,128)(2,1)}), bf16[32,32,128]{2,1,0:T(8,128)(2,1)S(1)}, u32[]{:S(2)}, u32[]{:S(2)}) async-start(bf16[32,32,128]{2,1,0:T(8,128)(2,1)} %shard_map.127), calls=%async_computation | async-start | bytes 524288 | tf_op jit(solution)/shard_map/all_to_all | solution.py:253
  13.5 3.9 %shard_map.128 = (bf16[640,32]{1,0:T(8,128)(2,1)}, bf16[640,64]{1,0:T(8,128)(2,1)}, f32[640,128]{1,0:T(8,128)}) custom-call(bf16[640,128]{1,0:T(8,128)(2,1)} %feats_ref.3, f32[1,128]{1,0:T(1,128)} %bitcast.24, bf16[3,32,128]{2,1,0:T(8,128)(2,1)} %bitcast.21, bf16[1,16]{1,0:T(2,128)(2,1)} %bitcast.25, bf16[16,640,128]{2,1,0:T(8,128)(2,1)} %apair_ref.1), custom_call_target="tpu_custom_call" | custom-call | flops 15728640 | bytes 2621440 | tf_op jit(solution)/shard_map/pallas_call | solution.py:284
  17.3 5.6 %all-to-all-done.msg_ref = bf16[32,32,128]{2,1,0:T(8,128)(2,1)S(1)} async-done(((bf16[32,32,128]{2,1,0:T(8,128)(2,1)}), bf16[32,32,128]{2,1,0:T(8,128)(2,1)S(1)}, u32[]{:S(2)}, u32[]{:S(2)}) %all-to-all-start) | async-done | bytes 262176 | tf_op jit(solution)/shard_map/all_to_all | solution.py:253
  23.7 4.4 %shard_map.129 = (bf16[32,32,80]{2,1,0:T(8,128)(2,1)}, f32[1,80]{1,0:T(1,128)}) custom-call(s32[1]{0:T(128)} %bitcast.1.row_ref, bf16[32,32,128]{2,1,0:T(8,128)(2,1)} %copy-done.25, bf16[640,32]{1,0:T(8,128)(2,1)} %get-tuple-element.57.q_ref, bf16[640,64]{1,0:T(8,128)(2,1)} %get-tuple-element.58.kv_ref, f32[640,128]{1,0:T(8,128)} %get-tuple-element.59.bias_ref), custom_call_target="tpu_custom_call" | custom-call | flops 115343360 | bytes 1048576 | tf_op jit(solution)/shard_map/pallas_call | solution.py:290
  28.1 4.1 %all-to-all-start.1 = ((bf16[32,32,80]{2,1,0:T(8,128)(2,1)}), bf16[32,32,80]{2,1,0:T(8,128)(2,1)S(1)}, u32[]{:S(2)}, u32[]{:S(2)}) async-start(bf16[32,32,80]{2,1,0:T(8,128)(2,1)} %get-tuple-element.61), calls=%async_computation.1 | async-start | bytes 524288 | tf_op jit(solution)/shard_map/all_to_all | solution.py:253
  32.2 10.4 %shard_map.130 = (bf16[4,80,640]{2,1,0:T(8,128)(2,1)}, bf16[4,80,640]{2,1,0:T(8,128)(2,1)}, bf16[4,80,640]{2,1,0:T(8,128)(2,1)}, bf16[4,80,640]{2,1,0:T(8,128)(2...) custom-call(s32[1]{0:T(128)} %bitcast.col_ref, ...), custom_call_target="tpu_custom_call" | custom-call | flops 419430400 | bytes 16384000 | tf_op jit(solution)/shard_map/pallas_call | solution.py:66
  42.7 7.2 %all_gather.15.sums_ref = bf16[128,80]{1,0:T(8,128)(2,1)S(1)} all-gather(bf16[32,80]{1,0:T(8,128)(2,1)S(1)} %shard_map.131), channel_id=1, replica_groups=mesh['row'=32,'col'=4] {'col'}, dimensions={0}, use_global_device_ids=true | all-gather | bytes 25600 | tf_op jit(solution)/shard_map/all_gather | solution.py:305
  50.8 2.9 %collective-permute-start = (bf16[80,384]{1,0:T(8,128)(2,1)S(1)}, bf16[80,384]{1,0:T(8,128)(2,1)S(1)}, u32[]{:S(2)}, u32[]{:S(2)}) collective-permute-start(bf16[80,384]{1,0:T(8,128)(2,1)S(1)} %get-tuple-element.80.own_ref), channel_id=1, source_target_pairs={{0,64},{4,68},{8,72},{12,76},{16,80},{20,84},{24,88},{28,92},{32,9... | collective-permute-start | bytes 184328 | tf_op jit(solution)/shard_map/ppermute | solution.py:318
  57.2 6.8 %all-to-all-start.2 = ((bf16[16,2,80,384]{3,2,1,0:T(8,128)(2,1)}), bf16[16,2,80,384]{3,2,1,0:T(8,128)(2,1)}, u32[]{:S(2)}, u32[]{:S(2)}) async-start(bf16[16,2,80,384]{3,2,1,0:T(8,128)(2,1)} %copy-done.1), calls=%async_computation.2 | async-start | bytes 3932160 | tf_op jit(solution)/shard_map/all_to_all | solution.py:327
  67.9 3.6 %collective-permute-done.2.w2_ref = bf16[192,768]{1,0:T(8,128)(2,1)S(1)} collective-permute-done((bf16[192,768]{1,0:T(8,128)(2,1)S(1)}, bf16[192,768]{1,0:T(8,128)(2,1)S(1)}, u32[]{:S(2)}, u32[]{:S(2)}) %collective-permute-start.2) | collective-permute-done | bytes 294944 | tf_op jit(solution)/shard_map/ppermute | solution.py:257
  71.5 3.9 %collective-permute-start.3 = (bf16[192,768]{1,0:T(8,128)(2,1)S(1)}, bf16[192,768]{1,0:T(8,128)(2,1)S(1)}, u32[]{:S(2)}, u32[]{:S(2)}) collective-permute-start(bf16[192,768]{1,0:T(8,128)(2,1)S(1)} %collective-permute-done.2.w2_ref), channel_id=1, source_target_pairs={{0,1},{1,0},{2,3},{3,2},{4,5},{5,4},{6,7},{7,6},{8,9},{9,8},{10,11... | collective-permute-start | bytes 884744 | tf_op jit(solution)/shard_map/ppermute | solution.py:257
  77.5 10.9 %all-to-all-done.2.kv_ref = bf16[16,2,80,384]{3,2,1,0:T(8,128)(2,1)} async-done(((bf16[16,2,80,384]{3,2,1,0:T(8,128)(2,1)}), bf16[16,2,80,384]{3,2,1,0:T(8,128)(2,1)}, u32[]{:S(2)}, u32[]{:S(2)}) %all-to-all-start.2) | async-done | bytes 1966112 | tf_op jit(solution)/shard_map/all_to_all | solution.py:327
  88.4 2.4 %collective-permute-done.6.bias3_ref = bf16[4,80,640]{2,1,0:T(8,128)(2,1)} collective-permute-done((bf16[4,80,640]{2,1,0:T(8,128)(2,1)}, bf16[4,80,640]{2,1,0:T(8,128)(2,1)}, u32[]{:S(2)}, u32[]{:S(2)}) %collective-permute-start.6) | collective-permute-done | bytes 409632 | tf_op jit(solution)/shard_map/ppermute | solution.py:257
  90.8 4.7 %shard_map.134 = bf16[80,192]{1,0:T(8,128)(2,1)S(1)} custom-call(s32[1]{0:T(128)} %bitcast.col_ref, s32[1]{0:T(128)S(6)} %select_n.5.half_ref, bf16[2,80,192]{2,1,0:T(8,128)(2,1)S(1)} %get-tuple-element.74.qg_ref, bf16[16,2,80,384]{3,2,1,0:T(8,128)(2,1)} %all-to-all-done.2.kv_ref, bf16[4,80,640]{2,1,0:T(8,128)(2,1)S(1)} %copy-done.4, ...), custom_call_target="tpu_custom_call" | custom-call | flops 157286400 | bytes 1638400 | tf_op jit(solution)/shard_map/pallas_call | solution.py:330
  95.6 8.0 %all-gather = bf16[320,192]{1,0:T(8,128)(2,1)S(1)} all-gather(bf16[80,192]{1,0:T(8,128)(2,1)S(1)} %shard_map.134), channel_id=2, replica_groups=mesh['row'=32,'col'=4] {'col'}, dimensions={0}, use_global_device_ids=true | all-gather | bytes 153600 | tf_op jit(solution)/shard_map/all_gather | solution.py:334
  105.3 2.8 %collective-permute-start.7 = (bf16[80,384]{1,0:T(8,128)(2,1)S(1)}, bf16[80,384]{1,0:T(8,128)(2,1)S(1)}, u32[]{:S(2)}, u32[]{:S(2)}) collective-permute-start(bf16[80,384]{1,0:T(8,128)(2,1)S(1)} %get-tuple-element.98.own_ref), channel_id=1, source_target_pairs={{0,64},{4,68},{8,72},{12,76},{16,80},{20,84},{24,88},{28,92},{32,9... | collective-permute-start | bytes 184328 | tf_op jit(solution)/shard_map/ppermute | solution.py:318
  108.1 2.2 %collective-permute-done.7.far_ref = bf16[80,384]{1,0:T(8,128)(2,1)S(1)} collective-permute-done((bf16[80,384]{1,0:T(8,128)(2,1)S(1)}, bf16[80,384]{1,0:T(8,128)(2,1)S(1)}, u32[]{:S(2)}, u32[]{:S(2)}) %collective-permute-start.7) | collective-permute-done | bytes 61472 | tf_op jit(solution)/shard_map/ppermute | solution.py:318
  111.8 3.8 %all-to-all-start.3 = ((bf16[16,2,80,384]{3,2,1,0:T(8,128)(2,1)}), bf16[16,2,80,384]{3,2,1,0:T(8,128)(2,1)S(1)}, u32[]{:S(2)}, u32[]{:S(2)}) async-start(bf16[16,2,80,384]{3,2,1,0:T(8,128)(2,1)} %copy-done.2), calls=%async_computation.3 | async-start | bytes 3932160 | tf_op jit(solution)/shard_map/all_to_all | solution.py:327
  119.4 3.6 %collective-permute-done.9.w2_ref = bf16[192,768]{1,0:T(8,128)(2,1)S(1)} collective-permute-done((bf16[192,768]{1,0:T(8,128)(2,1)S(1)}, bf16[192,768]{1,0:T(8,128)(2,1)S(1)}, u32[]{:S(2)}, u32[]{:S(2)}) %collective-permute-start.9) | collective-permute-done | bytes 294944 | tf_op jit(solution)/shard_map/ppermute | solution.py:257
  123.0 3.8 %collective-permute-start.10 = (bf16[192,768]{1,0:T(8,128)(2,1)S(1)}, bf16[192,768]{1,0:T(8,128)(2,1)S(1)}, u32[]{:S(2)}, u32[]{:S(2)}) collective-permute-start(bf16[192,768]{1,0:T(8,128)(2,1)S(1)} %collective-permute-done.9.w2_ref), channel_id=1, source_target_pairs={{0,1},{1,0},{2,3},{3,2},{4,5},{5,4},{6,7},{7,6},{8,9},{9,8},{10,11... | collective-permute-start | bytes 884744 | tf_op jit(solution)/shard_map/ppermute | solution.py:257
  129.0 11.0 %all-to-all-done.3.kv_ref = bf16[16,2,80,384]{3,2,1,0:T(8,128)(2,1)S(1)} async-done(((bf16[16,2,80,384]{3,2,1,0:T(8,128)(2,1)}), bf16[16,2,80,384]{3,2,1,0:T(8,128)(2,1)S(1)}, u32[]{:S(2)}, u32[]{:S(2)}) %all-to-all-start.3) | async-done | bytes 1966112 | tf_op jit(solution)/shard_map/all_to_all | solution.py:327
  140.0 2.3 %collective-permute-done.13.bias3_ref = bf16[4,80,640]{2,1,0:T(8,128)(2,1)} collective-permute-done((bf16[4,80,640]{2,1,0:T(8,128)(2,1)}, bf16[4,80,640]{2,1,0:T(8,128)(2,1)}, u32[]{:S(2)}, u32[]{:S(2)}) %collective-permute-start.13) | collective-permute-done | bytes 409632 | tf_op jit(solution)/shard_map/ppermute | solution.py:257
  142.3 4.0 %shard_map.137 = bf16[80,192]{1,0:T(8,128)(2,1)S(1)} custom-call(s32[1]{0:T(128)} %bitcast.col_ref, s32[1]{0:T(128)S(6)} %select_n.5.half_ref, bf16[2,80,192]{2,1,0:T(8,128)(2,1)S(1)} %get-tuple-element.92.qg_ref, bf16[16,2,80,384]{3,2,1,0:T(8,128)(2,1)S(1)} %all-to-all-done.3.kv_ref, bf16[4,80,640]{2,1,0:T(8,128)(2,1)S(1)} %copy-done.3, ...), custom_call_target="tpu_custom_call" | custom-call | flops 157286400 | bytes 1638400 | tf_op jit(solution)/shard_map/pallas_call | solution.py:330
  146.3 8.1 %all-gather.1 = bf16[320,192]{1,0:T(8,128)(2,1)S(1)} all-gather(bf16[80,192]{1,0:T(8,128)(2,1)S(1)} %shard_map.137), channel_id=3, replica_groups=mesh['row'=32,'col'=4] {'col'}, dimensions={0}, use_global_device_ids=true | all-gather | bytes 153600 | tf_op jit(solution)/shard_map/all_gather | solution.py:334
  (82 shorter events, 23.3 us)
Async XLA Ops:
  2.1 20.9 %all-to-all-start = ((bf16[32,32,128]{2,1,0:T(8,128)(2,1)}), bf16[32,32,128]{2,1,0:T(8,128)(2,1)S(1)}, u32[]{:S(2)}, u32[]{:S(2)}) async-start(bf16[32,32,128]{2,1,0:T(8,128)(2,1)} %shard_map.127), calls=%async_computation | async-start | bytes 524288 | tf_op jit(solution)/shard_map/all_to_all | solution.py:253
  28.1 14.6 %all-to-all-start.1 = ((bf16[32,32,80]{2,1,0:T(8,128)(2,1)}), bf16[32,32,80]{2,1,0:T(8,128)(2,1)S(1)}, u32[]{:S(2)}, u32[]{:S(2)}) async-start(bf16[32,32,80]{2,1,0:T(8,128)(2,1)} %get-tuple-element.61), calls=%async_computation.1 | async-start | bytes 524288 | tf_op jit(solution)/shard_map/all_to_all | solution.py:253
  32.2 17.7 %copy-start = (bf16[2,4,768,192]{2,3,1,0:T(8,128)(2,1)S(1)}, bf16[2,4,768,192]{2,3,1,0:T(8,128)(2,1)}, u32[]{:S(2)}) copy-start(bf16[2,4,768,192]{2,3,1,0:T(8,128)(2,1)} %param.22) | copy-start | bytes 7077892
  32.2 17.7 %copy-start.21 = (bf16[128,768]{1,0:T(8,128)(2,1)S(1)}, bf16[128,768]{1,0:T(8,128)(2,1)}, u32[]{:S(2)}) copy-start(bf16[128,768]{1,0:T(8,128)(2,1)} %w_pool_ref.1) | copy-start | bytes 589828
  32.2 17.7 %copy-start.22 = (bf16[80,768]{1,0:T(8,128)(2,1)S(1)}, bf16[80,768]{1,0:T(8,128)(2,1)}, u32[]{:S(2)}) copy-start(bf16[80,768]{1,0:T(8,128)(2,1)} %single_ref.1) | copy-start | bytes 368644
  32.2 17.7 %copy-start.23 = (f32[2,768]{1,0:T(2,128)S(1)}, f32[2,768]{1,0:T(2,128)}, u32[]{:S(2)}) copy-start(f32[2,768]{1,0:T(2,128)} %gain_ref.3) | copy-start | bytes 18436
  50.8 5.0 %collective-permute-start = (bf16[80,384]{1,0:T(8,128)(2,1)S(1)}, bf16[80,384]{1,0:T(8,128)(2,1)S(1)}, u32[]{:S(2)}, u32[]{:S(2)}) collective-permute-start(bf16[80,384]{1,0:T(8,128)(2,1)S(1)} %get-tuple-element.80.own_ref), channel_id=1, source_target_pairs={{0,64},{4,68},{8,72},{12,76},{16,80},{20,84},{24,88},{28,92},{32,9... | collective-permute-start | bytes 184328 | tf_op jit(solution)/shard_map/ppermute | solution.py:318
  57.2 33.6 %copy-start.4 = (bf16[4,80,640]{2,1,0:T(8,128)(2,1)S(1)}, bf16[4,80,640]{2,1,0:T(8,128)(2,1)}, u32[]{:S(2)}) copy-start(bf16[4,80,640]{2,1,0:T(8,128)(2,1)} %get-tuple-element.84.bias0_ref) | copy-start | bytes 1228804
  57.2 31.2 %all-to-all-start.2 = ((bf16[16,2,80,384]{3,2,1,0:T(8,128)(2,1)}), bf16[16,2,80,384]{3,2,1,0:T(8,128)(2,1)}, u32[]{:S(2)}, u32[]{:S(2)}) async-start(bf16[16,2,80,384]{3,2,1,0:T(8,128)(2,1)} %copy-done.1), calls=%async_computation.2 | async-start | bytes 3932160 | tf_op jit(solution)/shard_map/all_to_all | solution.py:327
  64.1 7.4 %collective-permute-start.2 = (bf16[192,768]{1,0:T(8,128)(2,1)S(1)}, bf16[192,768]{1,0:T(8,128)(2,1)S(1)}, u32[]{:S(2)}, u32[]{:S(2)}) collective-permute-start(bf16[192,768]{1,0:T(8,128)(2,1)S(1)} %get-tuple-element.82.w0_ref), channel_id=1, source_target_pairs={{0,2},{1,3},{2,0},{3,1},{4,6},{5,7},{6,4},{7,5},{8,10},{9,11},{10,... | collective-permute-start | bytes 884744 | tf_op jit(solution)/shard_map/ppermute | solution.py:257
  64.5 24.0 %collective-permute-start.4 = (bf16[4,80,640]{2,1,0:T(8,128)(2,1)}, bf16[4,80,640]{2,1,0:T(8,128)(2,1)}, u32[]{:S(2)}, u32[]{:S(2)}) collective-permute-start(bf16[4,80,640]{2,1,0:T(8,128)(2,1)} %get-tuple-element.85), channel_id=1, source_target_pairs={{0,1},{1,0},{2,3},{3,2},{4,5},{5,4},{6,7},{7,6},{8,9},{9,8},{10,11... | collective-permute-start | bytes 1228808 | tf_op jit(solution)/shard_map/ppermute | solution.py:257
  66.0 22.4 %collective-permute-start.5 = (bf16[4,80,640]{2,1,0:T(8,128)(2,1)}, bf16[4,80,640]{2,1,0:T(8,128)(2,1)}, u32[]{:S(2)}, u32[]{:S(2)}) collective-permute-start(bf16[4,80,640]{2,1,0:T(8,128)(2,1)} %get-tuple-element.86), channel_id=1, source_target_pairs={{0,2},{1,3},{2,0},{3,1},{4,6},{5,7},{6,4},{7,5},{8,10},{9,11},{10,... | collective-permute-start | bytes 1228808 | tf_op jit(solution)/shard_map/ppermute | solution.py:257
  67.2 23.7 %collective-permute-start.6 = (bf16[4,80,640]{2,1,0:T(8,128)(2,1)}, bf16[4,80,640]{2,1,0:T(8,128)(2,1)}, u32[]{:S(2)}, u32[]{:S(2)}) collective-permute-start(bf16[4,80,640]{2,1,0:T(8,128)(2,1)} %get-tuple-element.87), channel_id=1, source_target_pairs={{0,3},{1,2},{2,1},{3,0},{4,7},{5,6},{6,5},{7,4},{8,11},{9,10},{10,... | collective-permute-start | bytes 1228808 | tf_op jit(solution)/shard_map/ppermute | solution.py:257
  67.6 8.4 %collective-permute-start.1 = (bf16[192,768]{1,0:T(8,128)(2,1)S(1)}, bf16[192,768]{1,0:T(8,128)(2,1)S(1)}, u32[]{:S(2)}, u32[]{:S(2)}) collective-permute-start(bf16[192,768]{1,0:T(8,128)(2,1)S(1)} %get-tuple-element.82.w0_ref), channel_id=1, source_target_pairs={{0,1},{1,0},{2,3},{3,2},{4,5},{5,4},{6,7},{7,6},{8,9},{9,8},{10,11... | collective-permute-start | bytes 884744 | tf_op jit(solution)/shard_map/ppermute | solution.py:257
  71.5 5.3 %collective-permute-start.3 = (bf16[192,768]{1,0:T(8,128)(2,1)S(1)}, bf16[192,768]{1,0:T(8,128)(2,1)S(1)}, u32[]{:S(2)}, u32[]{:S(2)}) collective-permute-start(bf16[192,768]{1,0:T(8,128)(2,1)S(1)} %collective-permute-done.2.w2_ref), channel_id=1, source_target_pairs={{0,1},{1,0},{2,3},{3,2},{4,5},{5,4},{6,7},{7,6},{8,9},{9,8},{10,11... | collective-permute-start | bytes 884744 | tf_op jit(solution)/shard_map/ppermute | solution.py:257
  105.3 5.0 %collective-permute-start.7 = (bf16[80,384]{1,0:T(8,128)(2,1)S(1)}, bf16[80,384]{1,0:T(8,128)(2,1)S(1)}, u32[]{:S(2)}, u32[]{:S(2)}) collective-permute-start(bf16[80,384]{1,0:T(8,128)(2,1)S(1)} %get-tuple-element.98.own_ref), channel_id=1, source_target_pairs={{0,64},{4,68},{8,72},{12,76},{16,80},{20,84},{24,88},{28,92},{32,9... | collective-permute-start | bytes 184328 | tf_op jit(solution)/shard_map/ppermute | solution.py:318
  111.8 30.5 %copy-start.3 = (bf16[4,80,640]{2,1,0:T(8,128)(2,1)S(1)}, bf16[4,80,640]{2,1,0:T(8,128)(2,1)}, u32[]{:S(2)}) copy-start(bf16[4,80,640]{2,1,0:T(8,128)(2,1)} %get-tuple-element.102.bias0_ref) | copy-start | bytes 1228804
  111.8 28.2 %all-to-all-start.3 = ((bf16[16,2,80,384]{3,2,1,0:T(8,128)(2,1)}), bf16[16,2,80,384]{3,2,1,0:T(8,128)(2,1)S(1)}, u32[]{:S(2)}, u32[]{:S(2)}) async-start(bf16[16,2,80,384]{3,2,1,0:T(8,128)(2,1)} %copy-done.2), calls=%async_computation.3 | async-start | bytes 3932160 | tf_op jit(solution)/shard_map/all_to_all | solution.py:327
  115.6 7.4 %collective-permute-start.9 = (bf16[192,768]{1,0:T(8,128)(2,1)S(1)}, bf16[192,768]{1,0:T(8,128)(2,1)S(1)}, u32[]{:S(2)}, u32[]{:S(2)}) collective-permute-start(bf16[192,768]{1,0:T(8,128)(2,1)S(1)} %get-tuple-element.100.w0_ref), channel_id=1, source_target_pairs={{0,2},{1,3},{2,0},{3,1},{4,6},{5,7},{6,4},{7,5},{8,10},{9,11},{10,... | collective-permute-start | bytes 884744 | tf_op jit(solution)/shard_map/ppermute | solution.py:257
  116.0 23.9 %collective-permute-start.11 = (bf16[4,80,640]{2,1,0:T(8,128)(2,1)}, bf16[4,80,640]{2,1,0:T(8,128)(2,1)S(1)}, u32[]{:S(2)}, u32[]{:S(2)}) collective-permute-start(bf16[4,80,640]{2,1,0:T(8,128)(2,1)} %get-tuple-element.103), channel_id=1, source_target_pairs={{0,1},{1,0},{2,3},{3,2},{4,5},{5,4},{6,7},{7,6},{8,9},{9,8},{10,11... | collective-permute-start | bytes 1228808 | tf_op jit(solution)/shard_map/ppermute | solution.py:257
  117.5 22.5 %collective-permute-start.12 = (bf16[4,80,640]{2,1,0:T(8,128)(2,1)}, bf16[4,80,640]{2,1,0:T(8,128)(2,1)}, u32[]{:S(2)}, u32[]{:S(2)}) collective-permute-start(bf16[4,80,640]{2,1,0:T(8,128)(2,1)} %get-tuple-element.104), channel_id=1, source_target_pairs={{0,2},{1,3},{2,0},{3,1},{4,6},{5,7},{6,4},{7,5},{8,10},{9,11},{10,... | collective-permute-start | bytes 1228808 | tf_op jit(solution)/shard_map/ppermute | solution.py:257
  118.7 23.6 %collective-permute-start.13 = (bf16[4,80,640]{2,1,0:T(8,128)(2,1)}, bf16[4,80,640]{2,1,0:T(8,128)(2,1)}, u32[]{:S(2)}, u32[]{:S(2)}) collective-permute-start(bf16[4,80,640]{2,1,0:T(8,128)(2,1)} %get-tuple-element.105), channel_id=1, source_target_pairs={{0,3},{1,2},{2,1},{3,0},{4,7},{5,6},{6,5},{7,4},{8,11},{9,10},{10,... | collective-permute-start | bytes 1228808 | tf_op jit(solution)/shard_map/ppermute | solution.py:257
  119.1 8.4 %collective-permute-start.8 = (bf16[192,768]{1,0:T(8,128)(2,1)S(1)}, bf16[192,768]{1,0:T(8,128)(2,1)S(1)}, u32[]{:S(2)}, u32[]{:S(2)}) collective-permute-start(bf16[192,768]{1,0:T(8,128)(2,1)S(1)} %get-tuple-element.100.w0_ref), channel_id=1, source_target_pairs={{0,1},{1,0},{2,3},{3,2},{4,5},{5,4},{6,7},{7,6},{8,9},{9,8},{10,11... | collective-permute-start | bytes 884744 | tf_op jit(solution)/shard_map/ppermute | solution.py:257
  123.0 5.3 %collective-permute-start.10 = (bf16[192,768]{1,0:T(8,128)(2,1)S(1)}, bf16[192,768]{1,0:T(8,128)(2,1)S(1)}, u32[]{:S(2)}, u32[]{:S(2)}) collective-permute-start(bf16[192,768]{1,0:T(8,128)(2,1)S(1)} %collective-permute-done.9.w2_ref), channel_id=1, source_target_pairs={{0,1},{1,0},{2,3},{3,2},{4,5},{5,4},{6,7},{7,6},{8,9},{9,8},{10,11... | collective-permute-start | bytes 884744 | tf_op jit(solution)/shard_map/ppermute | solution.py:257
  (21 other events, 141.5 us)
